TPU v7x, 256 devices: a whole 4x4x8 slice. The times are simulated.
256 devices in a mesh: seq: 32 (over z, x), head: 8 (over y, core).
Axes of the slice: x: 4, y: 4, z: 8, core: 2. Of those that a mesh axis runs over, the one named last changes fastest.
Arguments:
- points: bfloat16 [65536, 512], P('seq'), may hold values from -12 to 12
- latents: bfloat16 [2048, 1536], replicated, may hold values from -12 to 12
- gain_in: float32 [512], replicated, may hold values from 0.1 to 1.9
- gain_lat: float32 [1536], replicated, may hold values from 0.1 to 1.9
- gain_self: float32 [1536], replicated, may hold values from 0.1 to 1.9
- cross_query: bfloat16 [1536, 1536], P(None, 'head'), may hold values from -1 to 1
- cross_key: bfloat16 [512, 1536], P(None, 'head'), may hold values from -1 to 1
- cross_value: bfloat16 [512, 1536], P(None, 'head'), may hold values from -0.25 to 0.25
- cross_out: bfloat16 [1536, 1536], P('head'), may hold values from -0.15625 to 0.15625
- self_query: bfloat16 [1536, 1536], P(None, 'head'), may hold values from -1 to 1
- latent_key_weight: bfloat16 [1536, 1536], P(None, 'head'), may hold values from -1 to 1
- self_value: bfloat16 [1536, 1536], P(None, 'head'), may hold values from -0.15625 to 0.15625
- self_out: bfloat16 [1536, 1536], P('head'), may hold values from -0.15625 to 0.15625
Outputs:
- encoded: bfloat16 [2048, 1536], P('seq', 'head')
All inputs are finite; a program needn't handle non-finite values.
Results may differ from a plain program's by a relative error of at most 0.012.
Values may be sent and summed in bfloat16 or wider, within the bound.
No kernel may reach another device: no remote copies, remote signals or barrier semaphores. Data moves between devices by JAX's collectives and lax.ppermute only.
A program may use at most 128 MiB of HBM per device.

v0:
```python
import functools
import jax
import jax.numpy as jnp
from jax import lax
from jax.experimental import pallas as pl
from jax.experimental.pallas import tpu as pltpu
from jax.sharding import PartitionSpec as P

NX = 4
NY = 4
NZ = 8
Z_GROUPS = [[z * NX + x for z in range(NZ)] for x in range(NX)]
SHIFTS = (1, NX - 1, 2)
FOREIGN = (2, 1, NX - 1)

HS = 96
AUG = 112
LANES = 256
CHUNK = 256
PIECE = 512
LOG2E = 1.4426950408889634
SAFE = 2.0**64
F32 = jnp.float32
BF16 = jnp.bfloat16
NT = (((1,), (1,)), ((), ()))
VMEM_LIMIT = 20 * 1024 * 1024
VMEM_WIDE = 58 * 1024 * 1024


def normed(values, gain):
    values = values.astype(F32)
    center = values - jnp.mean(values, axis=-1, keepdims=True)
    spread = jnp.mean(center * center, axis=-1, keepdims=True)
    return (center * lax.rsqrt(spread + 1e-05) * gain).astype(BF16)


def gain_row(gain):
    return jnp.concatenate([gain[i : i + 1, :] for i in range(gain.shape[0])], axis=1)


def split_pair(value):
    high = value.astype(BF16).astype(F32)
    return high, (value - high).astype(BF16).astype(F32)


def fetch(pairs, sems):
    return [pltpu.make_async_copy(src, dst, sems.at[i]) for i, (src, dst) in enumerate(pairs)]


def project_points(pbuf, gain, wk, wv, keys, values_t, xbuf, ready):
    one = (lax.broadcasted_iota(jnp.int32, (AUG - HS, PIECE), 0) == 0).astype(BF16)
    for i in range(pbuf.shape[0] // PIECE):
        ready(i)
        row = gain_row(gain)
        rows = pl.ds(i * PIECE, PIECE)
        for j in range(0, PIECE, 64):
            xbuf[j : j + 64, :] = normed(pbuf[i * PIECE + j : i * PIECE + j + 64, :], row)
        x = xbuf[...]
        keys[rows, :] = lax.dot_general(x, wk[...], NT, preferred_element_type=F32).astype(BF16)
        vt = lax.dot_general(wv[...], x, NT, preferred_element_type=F32).astype(BF16)
        for h in range(2):
            values_t[h, 0:HS, rows] = vt[h * HS : (h + 1) * HS]
            values_t[h, HS:AUG, rows] = one


def attend_units(queries, keys, values_t, sbuf, pbuf, emit):
    count = keys.shape[0]
    scale = LOG2E * HS ** (-0.5)
    chunks = count // CHUNK

    def score(u, c):
        rows = pl.ds(c * CHUNK, CHUNK)
        return lax.dot_general(keys[rows, :], queries[u][1], NT, preferred_element_type=F32)

    def first(u):
        s = score(u, 0)
        sbuf[u % 2] = s
        return split_pair(jnp.max(s, axis=0, keepdims=True) * scale)

    largest = jnp.zeros((1, LANES), F32)
    state = first(0)
    for u, (h, q) in enumerate(queries):
        high, low = state
        shift = high + low
        for c in range(chunks):
            s = sbuf[u % 2] if c == 0 else score(u, c)
            pbuf[u % 2, c * CHUNK : (c + 1) * CHUNK, :] = jnp.exp2(s * scale - shift).astype(BF16)
        acc = jnp.dot(values_t[h], pbuf[u % 2], preferred_element_type=F32)
        if u + 1 < len(queries):
            state = first(u + 1)
        emit(u, acc, high, low)
        largest = jnp.maximum(largest, acc[HS : HS + 1])
    return jnp.max(largest)


def attend_exact(h, q, keys, values_t):
    scale = LOG2E * HS ** (-0.5)
    chunks = keys.shape[0] // CHUNK

    def scores(c):
        rows = pl.ds(pl.multiple_of(c * CHUNK, CHUNK), CHUNK)
        s = lax.dot_general(keys[rows, :], q, NT, preferred_element_type=F32)
        return s * scale

    def largest(c, top):
        return jnp.maximum(top, jnp.max(scores(c), axis=0, keepdims=True))

    top = lax.fori_loop(0, chunks, largest, jnp.full((1, LANES), -jnp.inf, F32))
    high, low = split_pair(top)
    shift = high + low

    def add(c, acc):
        rows = pl.ds(pl.multiple_of(c * CHUNK, CHUNK), CHUNK)
        p = jnp.exp2(scores(c) - shift).astype(BF16)
        return acc + jnp.dot(values_t[h, :, rows], p, preferred_element_type=F32)

    acc = lax.fori_loop(0, chunks, add, jnp.zeros((AUG, LANES), F32))
    return acc, high, low


def with_stats(acc, total, high, low):
    total_high, total_low = split_pair(total)
    row = lax.broadcasted_iota(jnp.int32, (AUG - HS, acc.shape[1]), 0)
    stats = jnp.where(row == 0, total_high, 0.0)
    stats = jnp.where(row == 1, total_low, stats)
    stats = jnp.where(row == 2, high, stats)
    stats = jnp.where(row == 3, low, stats)
    return jnp.concatenate([acc[:HS], stats], axis=0).astype(BF16)


def attend_chunk(qbuf, keys, values_t, sbuf, pbuf, nbuf, out):
    rows = out.shape[2] // 2
    blocks = qbuf.shape[0] // LANES
    per = LANES // rows

    def query(j, h):
        start = j * LANES if isinstance(j, int) else pl.multiple_of(j * LANES, LANES)
        q = qbuf[pl.ds(start, LANES), :]
        lane = lax.broadcasted_iota(jnp.int32, q.shape, 1)
        return jnp.where((lane < HS) == (h == 0), q, jnp.zeros_like(q))

    def emit_at(j, h, acc, high, low):
        nbuf[h] = with_stats(acc, acc[HS : HS + 1], high, low)
        if h == 1:
            for i in range(per):
                lanes = slice(i * rows, (i + 1) * rows)
                out[j * per + i] = jnp.concatenate([nbuf[0, :, lanes], nbuf[1, :, lanes]], axis=1)

    queries = [(h, query(j, h)) for j in range(blocks) for h in range(2)]
    above = attend_units(
        queries, keys, values_t, sbuf, pbuf, lambda u, *r: emit_at(u // 2, u % 2, *r)
    )

    @pl.when(jnp.logical_not(above <= SAFE))
    def _():
        def again(j, carry):
            for h in range(2):
                emit_at(j, h, *attend_exact(h, query(j, h), keys, values_t))
            return carry

        lax.fori_loop(0, blocks, again, 0)


def norm_rows(lbuf, row, xbuf):
    rows = lbuf.shape[1]
    for z in range(lbuf.shape[0]):
        xbuf[z * rows : (z + 1) * rows, :] = normed(lbuf[z], row)


def project_query(xbuf, wq, qbuf):
    qbuf[...] = lax.dot_general(xbuf[...], wq[...], NT, preferred_element_type=F32).astype(BF16)


def encode_kernel(
    where, points, latents, gain_in, gain_lat, wk_in, wv_in, wq_in,
    out0, out1, out2, keys_out, values_out,
    pts, lbuf, gbuf, hbuf, wk, wv, wq, keys, values_t, ybuf, xbuf, qbuf, sbuf, pbuf, nbuf, sems,
):
    outs = (out0, out1, out2)
    pieces = [pl.ds(i * PIECE, PIECE) for i in range(pts.shape[0] // PIECE)]
    first = fetch(
        [(points.at[pieces[0], :], pts.at[pieces[0], :]), (gain_in, gbuf), (wk_in, wk), (wv_in, wv)]
        + [(points.at[rows, :], pts.at[rows, :]) for rows in pieces[1:]],
        sems,
    )
    later = fetch(
        [(gain_lat, hbuf), (wq_in, wq)]
        + [(latents.at[:, lax.rem(where[0] + k, NX)], lbuf.at[i]) for i, k in enumerate(FOREIGN)],
        sems.at[pl.ds(len(first), len(outs) + 2)],
    )
    back = fetch([(keys, keys_out), (values_t, values_out)], sems.at[pl.ds(0, 2)])
    for copy in first:
        copy.start()

    def ready(i):
        if i == 0:
            for copy in first[:4]:
                copy.wait()
            for copy in later:
                copy.start()
        else:
            first[3 + i].wait()

    project_points(pts, gbuf, wk, wv, keys, values_t, ybuf, ready)
    for copy in back:
        copy.start()
    later[0].wait()
    later[1].wait()
    row = gain_row(hbuf)
    for i, out in enumerate(outs):
        later[2 + i].wait()
        norm_rows(lbuf.at[i], row, xbuf)
        project_query(xbuf, wq, qbuf)
        attend_chunk(qbuf, keys, values_t, sbuf, pbuf, nbuf, out)
    for copy in back:
        copy.wait()


def own_kernel(
    where, latents, gain, wq_in, keys_in, values_in, out,
    lbuf, gbuf, wq, keys, values_t, xbuf, qbuf, sbuf, pbuf, nbuf, sems,
):
    copies = fetch(
        [(latents.at[:, where[0]], lbuf), (gain, gbuf), (wq_in, wq), (keys_in, keys), (values_in, values_t)],
        sems,
    )
    for copy in copies:
        copy.start()
    copies[0].wait()
    copies[1].wait()
    norm_rows(lbuf, gain_row(gbuf), xbuf)
    copies[2].wait()
    project_query(xbuf, wq, qbuf)
    copies[3].wait()
    copies[4].wait()
    attend_chunk(qbuf, keys, values_t, sbuf, pbuf, nbuf, out)


def anywhere():
    return pl.BlockSpec(memory_space=pl.ANY)


def whole():
    return pl.BlockSpec(memory_space=pltpu.VMEM)


def anywhere():
    return pl.BlockSpec(memory_space=pl.ANY)


def attend_scratch(n):
    return [
        pltpu.VMEM((2, CHUNK, LANES), F32),
        pltpu.VMEM((2, n, LANES), BF16),
        pltpu.VMEM((2, AUG, LANES), BF16),
    ]


def encode_call(where, points, latents, gain_in, gain_lat, wk, wv, wq):
    n, width = points.shape
    nz, nx, rows, depth = latents.shape
    part = jax.ShapeDtypeStruct((nz, AUG, 2 * rows), BF16)
    keys = jax.ShapeDtypeStruct((n, 2 * HS), BF16)
    values_t = jax.ShapeDtypeStruct((2, AUG, n), BF16)
    return pl.pallas_call(
        encode_kernel,
        out_shape=(part, part, part, keys, values_t),
        in_specs=[pl.BlockSpec(memory_space=pltpu.SMEM)] + [anywhere()] * 7,
        out_specs=(whole(), whole(), whole(), anywhere(), anywhere()),
        scratch_shapes=[
            pltpu.VMEM(points.shape, BF16),
            pltpu.VMEM((nx - 1, nz, rows, depth), BF16),
            pltpu.VMEM(gain_in.shape, F32),
            pltpu.VMEM(gain_lat.shape, F32),
            pltpu.VMEM(wk.shape, BF16),
            pltpu.VMEM(wv.shape, BF16),
            pltpu.VMEM(wq.shape, BF16),
            pltpu.VMEM(keys.shape, BF16),
            pltpu.VMEM(values_t.shape, BF16),
            pltpu.VMEM((PIECE, width), BF16),
            pltpu.VMEM((nz * rows, depth), BF16),
            pltpu.VMEM((nz * rows, 2 * HS), BF16),
        ]
        + attend_scratch(n)
        + [pltpu.SemaphoreType.DMA((n // PIECE + 8,))],
        compiler_params=pltpu.CompilerParams(vmem_limit_bytes=VMEM_WIDE),
        cost_estimate=pl.CostEstimate(
            flops=16 * 10**9, bytes_accessed=10**7, transcendentals=6 * 10**6
        ),
        name="encode",
    )(where, points, latents, gain_in, gain_lat, wk, wv, wq)


def own_call(where, latents, gain, wq, keys, values_t):
    nz, nx, rows, depth = latents.shape
    return pl.pallas_call(
        own_kernel,
        out_shape=jax.ShapeDtypeStruct((nz, AUG, 2 * rows), BF16),
        in_specs=[pl.BlockSpec(memory_space=pltpu.SMEM)] + [anywhere()] * 5,
        out_specs=whole(),
        scratch_shapes=[
            pltpu.VMEM((nz, rows, depth), BF16),
            pltpu.VMEM(gain.shape, F32),
            pltpu.VMEM(wq.shape, BF16),
            pltpu.VMEM(keys.shape, BF16),
            pltpu.VMEM(values_t.shape, BF16),
            pltpu.VMEM((nz * rows, depth), BF16),
            pltpu.VMEM((nz * rows, 2 * HS), BF16),
        ]
        + attend_scratch(keys.shape[0])
        + [pltpu.SemaphoreType.DMA((5,))],
        compiler_params=pltpu.CompilerParams(vmem_limit_bytes=VMEM_WIDE),
        cost_estimate=pl.CostEstimate(
            flops=4 * 10**9, bytes_accessed=5 * 10**6, transcendentals=2 * 10**6
        ),
        name="own",
    )(where, latents, gain, wq, keys, values_t)


def merge(parts):
    shifts = [p[HS + 2 : HS + 3] + p[HS + 3 : HS + 4] for p in parts]
    high, low = split_pair(functools.reduce(jnp.maximum, shifts))
    top = high + low
    acc = functools.reduce(jnp.add, [p * jnp.exp2(s - top) for p, s in zip(parts, shifts)])
    return acc, acc[HS : HS + 1] + acc[HS + 1 : HS + 2], high, low


def combine_kernel(a, b, c, d, out):
    for z in range(a.shape[0]):
        acc, total, high, low = merge([r[z].astype(F32) for r in (a, b, c, d)])
        out[z] = with_stats(acc, total, high, low)


def finish_kernel(*refs):
    out = refs[-1]
    parts = [r[i].astype(F32) for r in refs[:-1] for i in range(r.shape[0])]
    acc, total, _, _ = merge(parts)
    rows = out.shape[0]
    value = (acc[:HS] / total).T
    out[...] = jnp.concatenate([value[:rows], value[rows:]], axis=1).astype(BF16)


def near_kernel(a0, a1, a2, a3, w0, w1, w2, w3, out):
    total = None
    for a, w in ((a0, w0), (a1, w1), (a2, w2), (a3, w3)):
        term = jnp.dot(a[...], w[...], preferred_element_type=F32)
        total = term if total is None else total + term
    out[...] = total


def middle_kernel(latents, gain, own, other, wq, wk, wv, mid, q, kv):
    total = latents[...].astype(F32) + (own[...] + other[...])
    mid[...] = total
    x = normed(total, gain_row(gain))
    q[...] = lax.dot_general(x, wq[...], NT, preferred_element_type=F32).astype(BF16)
    k = lax.dot_general(x, wk[...], NT, preferred_element_type=F32).astype(BF16)
    v = lax.dot_general(x, wv[...], NT, preferred_element_type=F32).astype(BF16)
    both = jnp.concatenate([k, v], axis=1)
    for i in range(kv.shape[0]):
        kv[i] = both


def self_kernel(kv, q0, q1, q2, q3, out):
    scale = LOG2E * HS ** (-0.5)
    width = 2 * HS
    rows = q0.shape[0]
    keys = kv[:, 0:width]
    values_t = kv[:, width : 2 * width].astype(F32).T.astype(BF16)
    lane = lax.broadcasted_iota(jnp.int32, (rows, width), 1)
    first = lax.broadcasted_iota(jnp.int32, (HS, 2 * rows), 1) < rows
    for i, ref in enumerate((q0, q1, q2, q3)):
        q = ref[...]
        zero = jnp.zeros_like(q)
        both = jnp.concatenate([jnp.where(lane < HS, q, zero), jnp.where(lane < HS, zero, q)], axis=0)
        s = lax.dot_general(keys, both, NT, preferred_element_type=F32) * scale
        high, low = split_pair(jnp.max(s, axis=0, keepdims=True))
        p = jnp.exp2(s - (high + low))
        total = jnp.sum(p, axis=0, keepdims=True)
        n = jnp.dot(values_t, p.astype(BF16), preferred_element_type=F32)
        out[i] = with_stats(jnp.where(first, n[:HS], n[HS:]), total, high, low)


def output_kernel(attn, w, out):
    width = attn.shape[1]
    terms = jnp.dot(attn[...], w[...], preferred_element_type=F32)
    for i in range(out.shape[0]):
        out[i] = terms[:, i * width : (i + 1) * width].astype(BF16)


def add_kernel(mid, terms, out):
    total = mid[...]
    for i in range(terms.shape[0]):
        total = total + terms[i].astype(F32)
    out[...] = total.astype(BF16)


def plain_call(kernel, name, out_shape, *args, flops=6 * 10**9):
    moved = sum(a.size * a.dtype.itemsize for a in args)
    spec = lambda a: pl.BlockSpec(memory_space=pltpu.SMEM) if a.dtype == jnp.int32 else whole()
    return pl.pallas_call(
        kernel,
        out_shape=out_shape,
        in_specs=[spec(a) for a in args],
        out_specs=jax.tree.map(lambda _: whole(), out_shape),
        compiler_params=pltpu.CompilerParams(vmem_limit_bytes=VMEM_LIMIT),
        cost_estimate=pl.CostEstimate(flops=flops, bytes_accessed=moved, transcendentals=0),
        name=name,
    )(*args)


def permute_x(v, k):
    return lax.ppermute(
        v, "seq", [(i, (i // NX) * NX + (i % NX + k) % NX) for i in range(NX * NZ)]
    )


def permute_y(v, k):
    return lax.ppermute(v, "head", [(i, (i + 2 * k) % (2 * NY)) for i in range(2 * NY)])


def swap_cores(v):
    return lax.ppermute(v, "head", [(i, i ^ 1) for i in range(2 * NY)])


def gather_y(v):
    return [v] + [permute_y(v, k) for k in SHIFTS]


def body(
    points,
    latents,
    gain_in,
    gain_lat,
    gain_self,
    cross_query,
    cross_key,
    cross_value,
    cross_out,
    self_query,
    latent_key_weight,
    self_value,
    self_out,
):
    width = cross_query.shape[1]
    count, depth = latents.shape
    rows = count // (NX * NZ)
    seq = lax.axis_index("seq").astype(jnp.int32)
    head = lax.axis_index("head").astype(jnp.int32)
    part_shape = jax.ShapeDtypeStruct((NZ, AUG, 2 * rows), BF16)
    gains = [g.reshape(-1, 128) for g in (gain_in, gain_lat, gain_self)]

    out_near = gather_y(cross_out)
    latents_4d = latents.reshape(NZ, NX, rows, depth)
    x = (seq % NX).reshape(1)
    *sent, keys, values_t = encode_call(
        x, points, latents_4d, gains[0], gains[1], cross_key.T, cross_value.T, cross_query.T
    )
    parts = [permute_x(v, k) for v, k in zip(sent, FOREIGN)]
    part = own_call(x, latents_4d, gains[1], cross_query.T, keys, values_t)
    part = plain_call(combine_kernel, "combine", part_shape, part, *parts)
    lat_rows = lax.dynamic_slice_in_dim(latents, seq * rows, rows, 0)
    part = lax.all_to_all(part, "seq", 0, 0, axis_index_groups=Z_GROUPS)
    part, out_near, lat_rows = lax.optimization_barrier((part, out_near, lat_rows))
    block = jax.ShapeDtypeStruct((rows, width), BF16)
    cross_attn = plain_call(finish_kernel, "finish", block, part)
    own = plain_call(
        near_kernel, "near", jax.ShapeDtypeStruct((rows, depth), F32), *gather_y(cross_attn), *out_near
    )
    mid, squery, kv = plain_call(
        middle_kernel, "middle",
        (
            jax.ShapeDtypeStruct((rows, depth), F32),
            block,
            jax.ShapeDtypeStruct((NZ, rows, 2 * width), BF16),
        ),
        lat_rows, gains[2], own, swap_cores(own),
        self_query.T, latent_key_weight.T, self_value.T,
    )
    kv = lax.all_to_all(kv, "seq", 0, 0, axis_index_groups=Z_GROUPS)
    squeries = [squery] + [permute_x(squery, k) for k in SHIFTS]
    mid_cols = lax.dynamic_slice_in_dim(mid, head * width, width, 1)
    kv, mid_cols = lax.optimization_barrier((kv, mid_cols))
    part = plain_call(
        self_kernel, "self_part", jax.ShapeDtypeStruct((NX, AUG, 2 * rows), BF16),
        kv.reshape(NZ * rows, 2 * width), *squeries,
    )
    back = [part[0:1]] + [permute_x(part[i + 1 : i + 2], -k) for i, k in enumerate(SHIFTS)]
    self_attn = plain_call(finish_kernel, "finish_self", block, *back)
    terms = plain_call(
        output_kernel, "output", jax.ShapeDtypeStruct((2 * NY, rows, width), BF16), self_attn, self_out
    )
    terms = lax.all_to_all(terms, "head", 0, 0)
    return plain_call(add_kernel, "add", block, mid_cols, terms)


def solution(mesh):
    in_specs = (
        P("seq", None),
        P(),
        P(),
        P(),
        P(),
        P(None, "head"),
        P(None, "head"),
        P(None, "head"),
        P("head", None),
        P(None, "head"),
        P(None, "head"),
        P(None, "head"),
        P("head", None),
    )
    out_specs = P("seq", "head")
    return jax.shard_map(body, mesh=mesh, in_specs=in_specs, out_specs=out_specs, check_vma=False)
```

profile of v0, /device:TPU:1, one launch (start us, length us, event | category | flops | bytes accessed | tf_op | source)
XLA Modules:
  0.0 192.0 jit_solution(17824314564686422698)
XLA Ops:
  0.0 2.1 %collective-permute-start.3 = (bf16[192,1536]{1,0:T(8,128)(2,1)}, bf16[192,1536]{1,0:T(8,128)(2,1)S(1)}, u32[]{:S(2)}, u32[]{:S(2)}) collective-permute-start(bf16[192,1536]{1,0:T(8,128)(2,1)} %w0), channel_id=1, source_target_pairs={{0,2},{1,3},{2,4},{3,5},{4,6},{5,7},{6,0},{7,1},{8,10},{9,11},{10,... | collective-permute-start | bytes 1769480 | tf_op jit(solution)/shard_map/ppermute | solution.py:418
  2.1 1.4 collective-permute-start.4
  3.6 80.0 %encode.1 = (bf16[8,112,128]{2,1,0:T(8,128)(2,1)}, bf16[8,112,128]{2,1,0:T(8,128)(2,1)}, bf16[8,112,128]{2,1,0:T(8,128)(2,1)}, bf16[2048,192]{1,0:T(8,128)(2,1)}, bf16[2,112,2048]{2,1,0:T(8,128)(2,1)}) custom-call(s32[1]{0:T(128)} %bitcast.where, bf16[2048,512]{1,0:T(8,128)(2,1)} %points.1, bf16[8,4,64,1536]{3,2,1,0:T(8,128)(2,1)} %bitcast.17, ...), custom_call_target="tpu_custom_call" | custom-call | flops 16000000000 | bytes 10000000 | tf_op jit(solution)/shard_map/encode/pallas_call | solution.py:265
  83.5 2.8 %collective-permute-start = (bf16[8,112,128]{2,1,0:T(8,128)(2,1)}, bf16[8,112,128]{2,1,0:T(8,128)(2,1)S(1)}, u32[]{:S(2)}, u32[]{:S(2)}) collective-permute-start(bf16[8,112,128]{2,1,0:T(8,128)(2,1)} %get-tuple-element.23), channel_id=1, source_target_pairs={{0,16},{8,24},{16,0},{24,8},{32,48},{40,56},{48,32},{56,40},{64,80... | collective-permute-start | bytes 688136 | tf_op jit(solution)/shard_map/ppermute | solution.py:412
  86.4 0.3 collective-permute-start.1
  86.7 2.4 %collective-permute-start.2 = (bf16[8,112,128]{2,1,0:T(8,128)(2,1)}, bf16[8,112,128]{2,1,0:T(8,128)(2,1)S(1)}, u32[]{:S(2)}, u32[]{:S(2)}) collective-permute-start(bf16[8,112,128]{2,1,0:T(8,128)(2,1)} %get-tuple-element.25), channel_id=1, source_target_pairs={{0,24},{8,0},{16,8},{24,16},{32,56},{40,32},{48,40},{56,48},{64,88... | collective-permute-start | bytes 688136 | tf_op jit(solution)/shard_map/ppermute | solution.py:412
  89.1 0.0 copy-start
  89.1 27.6 %own.1.a = bf16[8,112,128]{2,1,0:T(8,128)(2,1)} custom-call(s32[1]{0:T(128)} %bitcast.where, bf16[8,4,64,1536]{3,2,1,0:T(8,128)(2,1)} %bitcast.18, f32[12,128]{1,0:T(8,128)} %bitcast.24, bf16[192,1536]{1,0:T(8,128)(2,1)} %bitcast.20, bf16[2048,192]{1,0:T(8,128)(2,1)} %get-tuple-element.21.keys_in, bf16[2,112,2048]{2,1,0:T(8,128)(2,1)} %get-tuple-element.22.values_in), custom_call_target="tpu_custom_call" | custom-call | flops 4000000000 | bytes 5000000 | tf_op jit(solution)/shard_map/own/pallas_call | solution.py:296
  116.7 0.0 collective-permute-done.b
  116.7 0.0 copy-done
  116.7 1.7 collective-permute-start.5
  118.4 0.0 collective-permute-done.1.c
  118.4 0.0 collective-permute-done.2.d
  118.4 0.0 copy-start.6
  118.4 0.9 copy-done.6
  119.4 1.0 combine.1
  120.3 7.3 %all-to-all-start = ((bf16[8,112,128]{2,1,0:T(8,128)(2,1)}), bf16[8,112,128]{2,1,0:T(8,128)(2,1)S(1)}, u32[]{:S(2)}, u32[]{:S(2)}) async-start(bf16[8,112,128]{2,1,0:T(8,128)(2,1)} %combine.1), calls=%async_computation | async-start | bytes 458752 | tf_op jit(solution)/shard_map/all_to_all | solution.py:462
  127.6 0.9 constant_dynamic-slice_fusion.1.latents
  128.6 0.0 collective-permute-done.3.w1
  128.6 0.0 collective-permute-done.4.w2
  128.6 2.6 %collective-permute-done.5.w3 = bf16[192,1536]{1,0:T(8,128)(2,1)S(1)} collective-permute-done((bf16[192,1536]{1,0:T(8,128)(2,1)S(1)}, bf16[192,1536]{1,0:T(8,128)(2,1)S(1)}, u32[]{:S(2)}, u32[]{:S(2)}) %collective-permute-start.5) | collective-permute-done | bytes 589856 | tf_op jit(solution)/shard_map/ppermute | solution.py:418
  131.1 5.5 %all-to-all-done.refs_0_ = bf16[8,112,128]{2,1,0:T(8,128)(2,1)S(1)} async-done(((bf16[8,112,128]{2,1,0:T(8,128)(2,1)}), bf16[8,112,128]{2,1,0:T(8,128)(2,1)S(1)}, u32[]{:S(2)}, u32[]{:S(2)}) %all-to-all-start) | async-done | bytes 229408 | tf_op jit(solution)/shard_map/all_to_all | solution.py:462
  136.6 0.2 finish.1.a0
  136.9 0.0 copy-start.1
  136.9 0.0 copy-start.2
  136.9 0.0 copy-start.3
  136.9 0.0 copy-start.5
  136.9 0.5 collective-permute-start.6
  137.4 2.3 %collective-permute-start.7 = (bf16[64,192]{1,0:T(8,128)(2,1)S(1)}, bf16[64,192]{1,0:T(8,128)(2,1)S(1)}, u32[]{:S(2)}, u32[]{:S(2)}) collective-permute-start(bf16[64,192]{1,0:T(8,128)(2,1)S(1)} %finish.1.a0), channel_id=1, source_target_pairs={{0,6},{1,7},{2,0},{3,1},{4,2},{5,3},{6,4},{7,5},{8,14},{9,15},{10,... | collective-permute-start | bytes 73736 | tf_op jit(solution)/shard_map/ppermute | solution.py:418
  139.7 0.1 collective-permute-start.8
  139.8 1.2 collective-permute-done.6.a1
  141.0 0.0 collective-permute-done.7.a2
  141.0 3.0 %collective-permute-done.8.a3 = bf16[64,192]{1,0:T(8,128)(2,1)S(1)} collective-permute-done((bf16[64,192]{1,0:T(8,128)(2,1)S(1)}, bf16[64,192]{1,0:T(8,128)(2,1)S(1)}, u32[]{:S(2)}, u32[]{:S(2)}) %collective-permute-start.8) | collective-permute-done | bytes 24608 | tf_op jit(solution)/shard_map/ppermute | solution.py:418
  143.9 0.5 near.1.own
  144.5 5.5 %collective-permute-start.9 = (f32[64,1536]{1,0:T(8,128)S(1)}, f32[64,1536]{1,0:T(8,128)S(1)}, u32[]{:S(2)}, u32[]{:S(2)}) collective-permute-start(f32[64,1536]{1,0:T(8,128)S(1)} %near.1.own), channel_id=1, source_target_pairs={{0,1},{1,0},{2,3},{3,2},{4,5},{5,4},{6,7},{7,6},{8,9},{9,8},{10,11... | collective-permute-start | bytes 1179656 | tf_op jit(solution)/shard_map/ppermute | solution.py:422
  150.0 1.3 collective-permute-done.9.other
  151.4 0.0 copy-done.1
  151.4 0.0 copy-done.2
  151.4 0.0 copy-done.3
  151.4 0.0 copy-done.5
  151.4 1.7 middle.1
  153.1 3.5 %all-to-all-start.1 = ((bf16[8,64,384]{2,1,0:T(8,128)(2,1)}), bf16[8,64,384]{2,1,0:T(8,128)(2,1)S(1)}, u32[]{:S(2)}, u32[]{:S(2)}) async-start(bf16[8,64,384]{2,1,0:T(8,128)(2,1)} %get-tuple-element.32), calls=%async_computation.1 | async-start | bytes 786432 | tf_op jit(solution)/shard_map/all_to_all | solution.py:479
  156.6 0.1 collective-permute-start.10
  156.6 2.7 %collective-permute-start.11 = (bf16[64,192]{1,0:T(8,128)(2,1)S(1)}, bf16[64,192]{1,0:T(8,128)(2,1)S(1)}, u32[]{:S(2)}, u32[]{:S(2)}) collective-permute-start(bf16[64,192]{1,0:T(8,128)(2,1)S(1)} %get-tuple-element.36.q0), channel_id=1, source_target_pairs={{0,24},{8,0},{16,8},{24,16},{32,56},{40,32},{48,40},{56,48},{64,88... | collective-permute-start | bytes 73736 | tf_op jit(solution)/shard_map/ppermute | solution.py:412
  159.3 0.0 collective-permute-start.12
  159.3 0.1 constant_dynamic-slice_fusion.mid
  159.4 12.2 %all-to-all-done.1 = bf16[8,64,384]{2,1,0:T(8,128)(2,1)S(1)} async-done(((bf16[8,64,384]{2,1,0:T(8,128)(2,1)}), bf16[8,64,384]{2,1,0:T(8,128)(2,1)S(1)}, u32[]{:S(2)}, u32[]{:S(2)}) %all-to-all-start.1) | async-done | bytes 393248 | tf_op jit(solution)/shard_map/all_to_all | solution.py:479
  171.6 0.0 collective-permute-done.10.q1
  171.6 0.0 collective-permute-done.11.q2
  171.6 0.0 collective-permute-done.12.q3
  171.6 1.5 self_part.1
  173.2 0.7 collective-permute-start.13
  173.9 0.8 collective-permute-start.14
  174.7 0.4 collective-permute-start.15
  175.1 0.8 collective-permute-done.13.refs_1_
  176.0 1.8 collective-permute-done.14.refs_2_
  177.8 1.1 collective-permute-done.15.refs_3_
  179.0 0.0 copy-start.4
  179.0 0.2 finish_self.1.attn
  179.2 0.9 copy-done.4
  180.0 0.3 output.1
  180.3 11.1 %all_to_all.15.terms = bf16[8,64,192]{2,1,0:T(8,128)(2,1)S(1)} all-to-all(bf16[8,64,192]{2,1,0:T(8,128)(2,1)S(1)} %output.1), channel_id=1, replica_groups=mesh['seq'=32,'head'=8] {'head'}, dimensions={0} | all-to-all | bytes 393216 | tf_op jit(solution)/shard_map/all_to_all | solution.py:492
  191.4 0.7 add.14
  (1 shorter events, 0.0 us)
Async XLA Ops:
  0.0 128.6 %collective-permute-start.3 = (bf16[192,1536]{1,0:T(8,128)(2,1)}, bf16[192,1536]{1,0:T(8,128)(2,1)S(1)}, u32[]{:S(2)}, u32[]{:S(2)}) collective-permute-start(bf16[192,1536]{1,0:T(8,128)(2,1)} %w0), channel_id=1, source_target_pairs={{0,2},{1,3},{2,4},{3,5},{4,6},{5,7},{6,0},{7,1},{8,10},{9,11},{10,... | collective-permute-start | bytes 1769480 | tf_op jit(solution)/shard_map/ppermute | solution.py:418
  2.1 126.4 %collective-permute-start.4 = (bf16[192,1536]{1,0:T(8,128)(2,1)}, bf16[192,1536]{1,0:T(8,128)(2,1)S(1)}, u32[]{:S(2)}, u32[]{:S(2)}) collective-permute-start(bf16[192,1536]{1,0:T(8,128)(2,1)} %w0), channel_id=1, source_target_pairs={{0,6},{1,7},{2,0},{3,1},{4,2},{5,3},{6,4},{7,5},{8,14},{9,15},{10,... | collective-permute-start | bytes 1769480 | tf_op jit(solution)/shard_map/ppermute | solution.py:418
  83.5 33.1 %collective-permute-start = (bf16[8,112,128]{2,1,0:T(8,128)(2,1)}, bf16[8,112,128]{2,1,0:T(8,128)(2,1)S(1)}, u32[]{:S(2)}, u32[]{:S(2)}) collective-permute-start(bf16[8,112,128]{2,1,0:T(8,128)(2,1)} %get-tuple-element.23), channel_id=1, source_target_pairs={{0,16},{8,24},{16,0},{24,8},{32,48},{40,56},{48,32},{56,40},{64,80... | collective-permute-start | bytes 688136 | tf_op jit(solution)/shard_map/ppermute | solution.py:412
  86.4 32.0 %collective-permute-start.1 = (bf16[8,112,128]{2,1,0:T(8,128)(2,1)}, bf16[8,112,128]{2,1,0:T(8,128)(2,1)S(1)}, u32[]{:S(2)}, u32[]{:S(2)}) collective-permute-start(bf16[8,112,128]{2,1,0:T(8,128)(2,1)} %get-tuple-element.24), channel_id=1, source_target_pairs={{0,8},{8,16},{16,24},{24,0},{32,40},{40,48},{48,56},{56,32},{64,72... | collective-permute-start | bytes 688136 | tf_op jit(solution)/shard_map/ppermute | solution.py:412
  86.7 31.7 %collective-permute-start.2 = (bf16[8,112,128]{2,1,0:T(8,128)(2,1)}, bf16[8,112,128]{2,1,0:T(8,128)(2,1)S(1)}, u32[]{:S(2)}, u32[]{:S(2)}) collective-permute-start(bf16[8,112,128]{2,1,0:T(8,128)(2,1)} %get-tuple-element.25), channel_id=1, source_target_pairs={{0,24},{8,0},{16,8},{24,16},{32,56},{40,32},{48,40},{56,48},{64,88... | collective-permute-start | bytes 688136 | tf_op jit(solution)/shard_map/ppermute | solution.py:412
  89.1 27.6 %copy-start = (bf16[192,1536]{1,0:T(8,128)(2,1)S(1)}, bf16[192,1536]{1,0:T(8,128)(2,1)}, u32[]{:S(2)}) copy-start(bf16[192,1536]{1,0:T(8,128)(2,1)} %w0) | copy-start | bytes 1769476
  116.7 14.4 %collective-permute-start.5 = (bf16[192,1536]{1,0:T(8,128)(2,1)S(1)}, bf16[192,1536]{1,0:T(8,128)(2,1)S(1)}, u32[]{:S(2)}, u32[]{:S(2)}) collective-permute-start(bf16[192,1536]{1,0:T(8,128)(2,1)S(1)} %copy-done), channel_id=1, source_target_pairs={{0,4},{1,5},{2,6},{3,7},{4,0},{5,1},{6,2},{7,3},{8,12},{9,13},{10,... | collective-permute-start | bytes 1769480 | tf_op jit(solution)/shard_map/ppermute | solution.py:418
  118.4 0.9 copy-start.6
  120.3 16.3 %all-to-all-start = ((bf16[8,112,128]{2,1,0:T(8,128)(2,1)}), bf16[8,112,128]{2,1,0:T(8,128)(2,1)S(1)}, u32[]{:S(2)}, u32[]{:S(2)}) async-start(bf16[8,112,128]{2,1,0:T(8,128)(2,1)} %combine.1), calls=%async_computation | async-start | bytes 458752 | tf_op jit(solution)/shard_map/all_to_all | solution.py:462
  136.9 14.5 %copy-start.1 = (bf16[1536,192]{0,1:T(8,128)(2,1)S(1)}, bf16[1536,192]{0,1:T(8,128)(2,1)}, u32[]{:S(2)}) copy-start(bf16[1536,192]{0,1:T(8,128)(2,1)} %param.22) | copy-start | bytes 1769476
  136.9 14.5 %copy-start.2 = (bf16[1536,192]{0,1:T(8,128)(2,1)S(1)}, bf16[1536,192]{0,1:T(8,128)(2,1)}, u32[]{:S(2)}) copy-start(bf16[1536,192]{0,1:T(8,128)(2,1)} %param.23) | copy-start | bytes 1769476
  136.9 14.5 %copy-start.3 = (bf16[1536,192]{0,1:T(8,128)(2,1)S(1)}, bf16[1536,192]{0,1:T(8,128)(2,1)}, u32[]{:S(2)}) copy-start(bf16[1536,192]{0,1:T(8,128)(2,1)} %param.24) | copy-start | bytes 1769476
  136.9 14.5 %copy-start.5 = (f32[1536]{0:T(1024)S(1)}, f32[1536]{0:T(1024)}, u32[]{:S(2)}) copy-start(f32[1536]{0:T(1024)} %param.17) | copy-start | bytes 18436
  136.9 4.1 %collective-permute-start.6 = (bf16[64,192]{1,0:T(8,128)(2,1)S(1)}, bf16[64,192]{1,0:T(8,128)(2,1)S(1)}, u32[]{:S(2)}, u32[]{:S(2)}) collective-permute-start(bf16[64,192]{1,0:T(8,128)(2,1)S(1)} %finish.1.a0), channel_id=1, source_target_pairs={{0,2},{1,3},{2,4},{3,5},{4,6},{5,7},{6,0},{7,1},{8,10},{9,11},{10,... | collective-permute-start | bytes 73736 | tf_op jit(solution)/shard_map/ppermute | solution.py:418
  137.4 3.6 %collective-permute-start.7 = (bf16[64,192]{1,0:T(8,128)(2,1)S(1)}, bf16[64,192]{1,0:T(8,128)(2,1)S(1)}, u32[]{:S(2)}, u32[]{:S(2)}) collective-permute-start(bf16[64,192]{1,0:T(8,128)(2,1)S(1)} %finish.1.a0), channel_id=1, source_target_pairs={{0,6},{1,7},{2,0},{3,1},{4,2},{5,3},{6,4},{7,5},{8,14},{9,15},{10,... | collective-permute-start | bytes 73736 | tf_op jit(solution)/shard_map/ppermute | solution.py:418
  139.7 4.3 %collective-permute-start.8 = (bf16[64,192]{1,0:T(8,128)(2,1)S(1)}, bf16[64,192]{1,0:T(8,128)(2,1)S(1)}, u32[]{:S(2)}, u32[]{:S(2)}) collective-permute-start(bf16[64,192]{1,0:T(8,128)(2,1)S(1)} %finish.1.a0), channel_id=1, source_target_pairs={{0,4},{1,5},{2,6},{3,7},{4,0},{5,1},{6,2},{7,3},{8,12},{9,13},{10,... | collective-permute-start | bytes 73736 | tf_op jit(solution)/shard_map/ppermute | solution.py:418
  144.5 6.9 %collective-permute-start.9 = (f32[64,1536]{1,0:T(8,128)S(1)}, f32[64,1536]{1,0:T(8,128)S(1)}, u32[]{:S(2)}, u32[]{:S(2)}) collective-permute-start(f32[64,1536]{1,0:T(8,128)S(1)} %near.1.own), channel_id=1, source_target_pairs={{0,1},{1,0},{2,3},{3,2},{4,5},{5,4},{6,7},{7,6},{8,9},{9,8},{10,11... | collective-permute-start | bytes 1179656 | tf_op jit(solution)/shard_map/ppermute | solution.py:422
  153.1 18.5 %all-to-all-start.1 = ((bf16[8,64,384]{2,1,0:T(8,128)(2,1)}), bf16[8,64,384]{2,1,0:T(8,128)(2,1)S(1)}, u32[]{:S(2)}, u32[]{:S(2)}) async-start(bf16[8,64,384]{2,1,0:T(8,128)(2,1)} %get-tuple-element.32), calls=%async_computation.1 | async-start | bytes 786432 | tf_op jit(solution)/shard_map/all_to_all | solution.py:479
  156.6 15.1 %collective-permute-start.10 = (bf16[64,192]{1,0:T(8,128)(2,1)S(1)}, bf16[64,192]{1,0:T(8,128)(2,1)S(1)}, u32[]{:S(2)}, u32[]{:S(2)}) collective-permute-start(bf16[64,192]{1,0:T(8,128)(2,1)S(1)} %get-tuple-element.36.q0), channel_id=1, source_target_pairs={{0,8},{8,16},{16,24},{24,0},{32,40},{40,48},{48,56},{56,32},{64,72... | collective-permute-start | bytes 73736 | tf_op jit(solution)/shard_map/ppermute | solution.py:412
  156.6 15.0 %collective-permute-start.11 = (bf16[64,192]{1,0:T(8,128)(2,1)S(1)}, bf16[64,192]{1,0:T(8,128)(2,1)S(1)}, u32[]{:S(2)}, u32[]{:S(2)}) collective-permute-start(bf16[64,192]{1,0:T(8,128)(2,1)S(1)} %get-tuple-element.36.q0), channel_id=1, source_target_pairs={{0,24},{8,0},{16,8},{24,16},{32,56},{40,32},{48,40},{56,48},{64,88... | collective-permute-start | bytes 73736 | tf_op jit(solution)/shard_map/ppermute | solution.py:412
  159.3 12.3 %collective-permute-start.12 = (bf16[64,192]{1,0:T(8,128)(2,1)S(1)}, bf16[64,192]{1,0:T(8,128)(2,1)S(1)}, u32[]{:S(2)}, u32[]{:S(2)}) collective-permute-start(bf16[64,192]{1,0:T(8,128)(2,1)S(1)} %get-tuple-element.36.q0), channel_id=1, source_target_pairs={{0,16},{8,24},{16,0},{24,8},{32,48},{40,56},{48,32},{56,40},{64,80... | collective-permute-start | bytes 73736 | tf_op jit(solution)/shard_map/ppermute | solution.py:412
  173.2 2.8 %collective-permute-start.13 = (bf16[1,112,128]{2,1,0:T(8,128)(2,1)S(1)}, bf16[1,112,128]{2,1,0:T(8,128)(2,1)S(1)}, u32[]{:S(2)}, u32[]{:S(2)}) collective-permute-start(bf16[1,112,128]{2,1,0:T(8,128)(2,1)S(1)} %get-tuple-element.39), channel_id=1, source_target_pairs={{0,24},{8,0},{16,8},{24,16},{32,56},{40,32},{48,40},{56,48},{64,88... | collective-permute-start | bytes 86024 | tf_op jit(solution)/shard_map/ppermute | solution.py:412
  173.9 3.9 %collective-permute-start.14 = (bf16[1,112,128]{2,1,0:T(8,128)(2,1)S(1)}, bf16[1,112,128]{2,1,0:T(8,128)(2,1)S(1)}, u32[]{:S(2)}, u32[]{:S(2)}) collective-permute-start(bf16[1,112,128]{2,1,0:T(8,128)(2,1)S(1)} %get-tuple-element.38), channel_id=1, source_target_pairs={{0,8},{8,16},{16,24},{24,0},{32,40},{40,48},{48,56},{56,32},{64,72... | collective-permute-start | bytes 86024 | tf_op jit(solution)/shard_map/ppermute | solution.py:412
  174.7 4.2 %collective-permute-start.15 = (bf16[1,112,128]{2,1,0:T(8,128)(2,1)S(1)}, bf16[1,112,128]{2,1,0:T(8,128)(2,1)S(1)}, u32[]{:S(2)}, u32[]{:S(2)}) collective-permute-start(bf16[1,112,128]{2,1,0:T(8,128)(2,1)S(1)} %get-tuple-element.37), channel_id=1, source_target_pairs={{0,16},{8,24},{16,0},{24,8},{32,48},{40,56},{48,32},{56,40},{64,80... | collective-permute-start | bytes 86024 | tf_op jit(solution)/shard_map/ppermute | solution.py:412
  179.0 1.1 copy-start.4
where the time goes:
time: 193 us; the launch traced here: 192 us
  Pallas kernels  114 us (59%)
  starting transfers between devices  34.7 us (18%)
  waiting for transfers between devices  29.6 us (15%)
  blocking collectives  11.1 us (6%)
  local copies, waits for them, and re-layouts  2.86 us (1%)
    pallas_call x1, Pallas kernels, encode_call(): pl.pallas_call(encode_kernel, out_shape=(part, part, part, keys, values_t...  80 us
    pallas_call x1, Pallas kernels, own_call(): pl.pallas_call(own_kernel, out_shape=jax.ShapeDtypeStruct((nz, AUG, 2 * r...  27.6 us
    all_to_all x1, waiting for transfers between devices, body(): kv = lax.all_to_all(kv, 'seq', 0, 0, axis_index_groups=Z_GROUPS)  12.2 us
    all_to_all x1, blocking collectives, body(): terms = lax.all_to_all(terms, 'head', 0, 0)  11.1 us
    ppermute x9, starting transfers between devices, permute_x(): lax.ppermute(v, 'seq', [(i, i // NX * NX + (i % NX + k) % NX) for i in ra...  10.3 us
    ppermute x6, starting transfers between devices, permute_y(): lax.ppermute(v, 'head', [(i, (i + 2 * k) % (2 * NY)) for i in range(2 * N...  8.13 us
    all_to_all x1, starting transfers between devices, body(): part = lax.all_to_all(part, 'seq', 0, 0, axis_index_groups=Z_GROUPS)  7.3 us
    ppermute x6, waiting for transfers between devices, permute_y(): lax.ppermute(v, 'head', [(i, (i + 2 * k) % (2 * NY)) for i in range(2 * N...  6.71 us
  transfers between devices with their start and end apart: 18, of which 9 were waited for; matrix products, arithmetic and copies ran while one was open for 1% of the time, Pallas kernels for 57%

commit v1 on v0

--- a/solution.py
+++ b/solution.py
@@ -48,19 +48,19 @@
 
 
 def project_points(pbuf, gain, wk, wv, keys, values_t, xbuf, ready):
-    one = (lax.broadcasted_iota(jnp.int32, (AUG - HS, PIECE), 0) == 0).astype(BF16)
     for i in range(pbuf.shape[0] // PIECE):
         ready(i)
         row = gain_row(gain)
-        rows = pl.ds(i * PIECE, PIECE)
-        for j in range(0, PIECE, 64):
-            xbuf[j : j + 64, :] = normed(pbuf[i * PIECE + j : i * PIECE + j + 64, :], row)
-        x = xbuf[...]
-        keys[rows, :] = lax.dot_general(x, wk[...], NT, preferred_element_type=F32).astype(BF16)
-        vt = lax.dot_general(wv[...], x, NT, preferred_element_type=F32).astype(BF16)
-        for h in range(2):
-            values_t[h, 0:HS, rows] = vt[h * HS : (h + 1) * HS]
-            values_t[h, HS:AUG, rows] = one
+        for j in range(i * PIECE, (i + 1) * PIECE, 64):
+            xbuf[j : j + 64, :] = normed(pbuf[j : j + 64, :], row)
+    x = xbuf[...]
+    keys[...] = lax.dot_general(x, wk[...], NT, preferred_element_type=F32).astype(BF16)
+    vt = lax.dot_general(wv[...], x, NT, preferred_element_type=F32).astype(BF16)
+    for h in range(2):
+        values_t[h, 0:HS, :] = vt[h * HS : (h + 1) * HS]
+    one = lax.broadcasted_iota(jnp.int32, (AUG - HS, pbuf.shape[0]), 0) == 0
+    for h in range(2):
+        values_t[h, HS:AUG, :] = one.astype(BF16)
 
 
 def attend_units(queries, keys, values_t, sbuf, pbuf, emit):
@@ -128,10 +128,8 @@
     return jnp.concatenate([acc[:HS], stats], axis=0).astype(BF16)
 
 
-def attend_chunk(qbuf, keys, values_t, sbuf, pbuf, nbuf, out):
-    rows = out.shape[2] // 2
+def attend_chunk(qbuf, keys, values_t, sbuf, pbuf, out):
     blocks = qbuf.shape[0] // LANES
-    per = LANES // rows
 
     def query(j, h):
         start = j * LANES if isinstance(j, int) else pl.multiple_of(j * LANES, LANES)
@@ -140,11 +138,7 @@
         return jnp.where((lane < HS) == (h == 0), q, jnp.zeros_like(q))
 
     def emit_at(j, h, acc, high, low):
-        nbuf[h] = with_stats(acc, acc[HS : HS + 1], high, low)
-        if h == 1:
-            for i in range(per):
-                lanes = slice(i * rows, (i + 1) * rows)
-                out[j * per + i] = jnp.concatenate([nbuf[0, :, lanes], nbuf[1, :, lanes]], axis=1)
+        out[j, h] = with_stats(acc, acc[HS : HS + 1], high, low)
 
     queries = [(h, query(j, h)) for j in range(blocks) for h in range(2)]
     above = attend_units(
@@ -162,9 +156,15 @@
 
 
 def norm_rows(lbuf, row, xbuf):
-    rows = lbuf.shape[1]
+    rows, width = lbuf.shape[1], lbuf.shape[2]
     for z in range(lbuf.shape[0]):
-        xbuf[z * rows : (z + 1) * rows, :] = normed(lbuf[z], row)
+        part = pl.ds(z * rows, rows)
+        x = lbuf[z].astype(F32)
+        off = x - x[:, 0:1]
+        mean = jnp.sum(off, axis=-1, keepdims=True) * (1.0 / width)
+        spread = jnp.sum(off * off, axis=-1, keepdims=True) * (1.0 / width) - mean * mean
+        factor = lax.rsqrt(jnp.maximum(spread, 0.0) + 1e-05)
+        xbuf[part, :] = ((off - mean) * factor * row).astype(BF16)
 
 
 def project_query(xbuf, wq, qbuf):
@@ -174,7 +174,7 @@
 def encode_kernel(
     where, points, latents, gain_in, gain_lat, wk_in, wv_in, wq_in,
     out0, out1, out2, keys_out, values_out,
-    pts, lbuf, gbuf, hbuf, wk, wv, wq, keys, values_t, ybuf, xbuf, qbuf, sbuf, pbuf, nbuf, sems,
+    pts, lbuf, gbuf, hbuf, wk, wv, wq, keys, values_t, ybuf, xbuf, qbuf, sbuf, pbuf, sems,
 ):
     outs = (out0, out1, out2)
     pieces = [pl.ds(i * PIECE, PIECE) for i in range(pts.shape[0] // PIECE)]
@@ -211,14 +211,14 @@
         later[2 + i].wait()
         norm_rows(lbuf.at[i], row, xbuf)
         project_query(xbuf, wq, qbuf)
-        attend_chunk(qbuf, keys, values_t, sbuf, pbuf, nbuf, out)
+        attend_chunk(qbuf, keys, values_t, sbuf, pbuf, out)
     for copy in back:
         copy.wait()
 
 
 def own_kernel(
     where, latents, gain, wq_in, keys_in, values_in, out,
-    lbuf, gbuf, wq, keys, values_t, xbuf, qbuf, sbuf, pbuf, nbuf, sems,
+    lbuf, gbuf, wq, keys, values_t, xbuf, qbuf, sbuf, pbuf, sems,
 ):
     copies = fetch(
         [(latents.at[:, where[0]], lbuf), (gain, gbuf), (wq_in, wq), (keys_in, keys), (values_in, values_t)],
@@ -233,7 +233,7 @@
     project_query(xbuf, wq, qbuf)
     copies[3].wait()
     copies[4].wait()
-    attend_chunk(qbuf, keys, values_t, sbuf, pbuf, nbuf, out)
+    attend_chunk(qbuf, keys, values_t, sbuf, pbuf, out)
 
 
 def anywhere():
@@ -252,14 +252,13 @@
     return [
         pltpu.VMEM((2, CHUNK, LANES), F32),
         pltpu.VMEM((2, n, LANES), BF16),
-        pltpu.VMEM((2, AUG, LANES), BF16),
     ]
 
 
 def encode_call(where, points, latents, gain_in, gain_lat, wk, wv, wq):
     n, width = points.shape
     nz, nx, rows, depth = latents.shape
-    part = jax.ShapeDtypeStruct((nz, AUG, 2 * rows), BF16)
+    part = jax.ShapeDtypeStruct((nz * rows // LANES, 2, AUG, LANES), BF16)
     keys = jax.ShapeDtypeStruct((n, 2 * HS), BF16)
     values_t = jax.ShapeDtypeStruct((2, AUG, n), BF16)
     return pl.pallas_call(
@@ -277,7 +276,7 @@
             pltpu.VMEM(wq.shape, BF16),
             pltpu.VMEM(keys.shape, BF16),
             pltpu.VMEM(values_t.shape, BF16),
-            pltpu.VMEM((PIECE, width), BF16),
+            pltpu.VMEM(points.shape, BF16),
             pltpu.VMEM((nz * rows, depth), BF16),
             pltpu.VMEM((nz * rows, 2 * HS), BF16),
         ]
@@ -295,7 +294,7 @@
     nz, nx, rows, depth = latents.shape
     return pl.pallas_call(
         own_kernel,
-        out_shape=jax.ShapeDtypeStruct((nz, AUG, 2 * rows), BF16),
+        out_shape=jax.ShapeDtypeStruct((nz * rows // LANES, 2, AUG, LANES), BF16),
         in_specs=[pl.BlockSpec(memory_space=pltpu.SMEM)] + [anywhere()] * 5,
         out_specs=whole(),
         scratch_shapes=[
@@ -326,18 +325,27 @@
 
 
 def combine_kernel(a, b, c, d, out):
-    for z in range(a.shape[0]):
-        acc, total, high, low = merge([r[z].astype(F32) for r in (a, b, c, d)])
-        out[z] = with_stats(acc, total, high, low)
-
-
-def finish_kernel(*refs):
-    out = refs[-1]
-    parts = [r[i].astype(F32) for r in refs[:-1] for i in range(r.shape[0])]
+    rows = out.shape[2] // 2
+    per = LANES // rows
+    for j in range(a.shape[0]):
+        packed = []
+        for h in range(2):
+            acc, total, high, low = merge([r[j, h].astype(F32) for r in (a, b, c, d)])
+            packed.append(with_stats(acc, total, high, low))
+        for i in range(per):
+            lanes = slice(i * rows, (i + 1) * rows)
+            out[j * per + i] = jnp.concatenate([p[:, lanes] for p in packed], axis=1)
+
+
+def finish(refs, rows):
+    parts = [r[i].astype(F32) for r in refs for i in range(r.shape[0])]
     acc, total, _, _ = merge(parts)
-    rows = out.shape[0]
     value = (acc[:HS] / total).T
-    out[...] = jnp.concatenate([value[:rows], value[rows:]], axis=1).astype(BF16)
+    return jnp.concatenate([value[:rows], value[rows:]], axis=1).astype(BF16)
+
+
+def finish_kernel(part, out):
+    out[...] = finish([part], out.shape[0])
 
 
 def near_kernel(a0, a1, a2, a3, w0, w1, w2, w3, out):
@@ -380,10 +388,11 @@
         out[i] = with_stats(jnp.where(first, n[:HS], n[HS:]), total, high, low)
 
 
-def output_kernel(attn, w, out):
-    width = attn.shape[1]
-    terms = jnp.dot(attn[...], w[...], preferred_element_type=F32)
-    for i in range(out.shape[0]):
+def output_kernel(p0, p1, p2, p3, w, out):
+    count, rows, width = out.shape
+    attn = finish([p0, p1, p2, p3], rows)
+    terms = jnp.dot(attn, w[...], preferred_element_type=F32)
+    for i in range(count):
         out[i] = terms[:, i * width : (i + 1) * width].astype(BF16)
 
 
@@ -449,7 +458,7 @@
     part_shape = jax.ShapeDtypeStruct((NZ, AUG, 2 * rows), BF16)
     gains = [g.reshape(-1, 128) for g in (gain_in, gain_lat, gain_self)]
 
-    out_near = gather_y(cross_out)
+    out_near = [cross_out] + [permute_y(cross_out, k) for k in SHIFTS[:2]]
     latents_4d = latents.reshape(NZ, NX, rows, depth)
     x = (seq % NX).reshape(1)
     *sent, keys, values_t = encode_call(
@@ -458,6 +467,8 @@
     parts = [permute_x(v, k) for v, k in zip(sent, FOREIGN)]
     part = own_call(x, latents_4d, gains[1], cross_query.T, keys, values_t)
     part = plain_call(combine_kernel, "combine", part_shape, part, *parts)
+    part, last = lax.optimization_barrier((part, cross_out))
+    out_near.append(permute_y(last, SHIFTS[2]))
     lat_rows = lax.dynamic_slice_in_dim(latents, seq * rows, rows, 0)
     part = lax.all_to_all(part, "seq", 0, 0, axis_index_groups=Z_GROUPS)
     part, out_near, lat_rows = lax.optimization_barrier((part, out_near, lat_rows))
@@ -485,9 +496,8 @@
         kv.reshape(NZ * rows, 2 * width), *squeries,
     )
     back = [part[0:1]] + [permute_x(part[i + 1 : i + 2], -k) for i, k in enumerate(SHIFTS)]
-    self_attn = plain_call(finish_kernel, "finish_self", block, *back)
     terms = plain_call(
-        output_kernel, "output", jax.ShapeDtypeStruct((2 * NY, rows, width), BF16), self_attn, self_out
+        output_kernel, "output", jax.ShapeDtypeStruct((2 * NY, rows, width), BF16), *back, self_out
     )
     terms = lax.all_to_all(terms, "head", 0, 0)
     return plain_call(add_kernel, "add", block, mid_cols, terms)

time: 193 us -> 190 us (0.984)
  Pallas kernels: 114 us -> 29.7 us
  starting transfers between devices: 34.7 us -> 115 us
  waiting for transfers between devices: 29.6 us -> 32.9 us
    pallas_call x1, Pallas kernels: 80 us -> 16.8 us  [encode_call(): pl.pallas_call(encode_kernel, out_shape=(part, part, part, keys, values_t...]
    ppermute x9, starting transfers between devices: 10.3 us -> 69.9 us  [permute_x(): lax.ppermute(v, 'seq', [(i, i // NX * NX + (i % NX + k) % NX) for i in ra...]
    pallas_call x1, Pallas kernels: 27.6 us -> 6.83 us  [own_call(): pl.pallas_call(own_kernel, out_shape=jax.ShapeDtypeStruct((nz * rows // L...]
    all_to_all x1, starting transfers between devices: 7.3 us -> 27.9 us  [body(): part = lax.all_to_all(part, 'seq', 0, 0, axis_index_groups=Z_GROUPS)]
    ppermute x9, waiting for transfers between devices: 3.82 us -> 7.11 us  [permute_x(): lax.ppermute(v, 'seq', [(i, i // NX * NX + (i % NX + k) % NX) for i in ra...]
    all_to_all x1, waiting for transfers between devices: 5.52 us -> 8.07 us  [body(): part = lax.all_to_all(part, 'seq', 0, 0, axis_index_groups=Z_GROUPS)]
    ppermute x6, waiting for transfers between devices: 6.71 us -> 4.16 us  [permute_y(): lax.ppermute(v, 'head', [(i, (i + 2 * k) % (2 * NY)) for i in range(2 * N...]
    pallas_call x8 -> x7, Pallas kernels: 6.04 us -> 6.1 us  [plain_call(): pl.pallas_call(kernel, out_shape=out_shape, in_specs=[spec(a) for a in ar...]
  transfers between devices with their start and end apart: 18 -> 18, of which waited for: 9 -> 9; matrix products, arithmetic and copies ran while one was open for 1% -> 1% of each run, Pallas kernels for 57% -> 13%
where the time goes in v1:
time: 190 us; the launch traced here: 191 us
  starting transfers between devices  115 us (61%)
  waiting for transfers between devices  32.9 us (17%)
  Pallas kernels  29.7 us (16%)
  blocking collectives  11.1 us (6%)
  local copies, waits for them, and re-layouts  2.01 us (1%)
    ppermute x9, starting transfers between devices, permute_x(): lax.ppermute(v, 'seq', [(i, i // NX * NX + (i % NX + k) % NX) for i in ra...  69.9 us
    all_to_all x1, starting transfers between devices, body(): part = lax.all_to_all(part, 'seq', 0, 0, axis_index_groups=Z_GROUPS)  27.9 us
    pallas_call x1, Pallas kernels, encode_call(): pl.pallas_call(encode_kernel, out_shape=(part, part, part, keys, values_t...  16.8 us
    all_to_all x1, waiting for transfers between devices, body(): kv = lax.all_to_all(kv, 'seq', 0, 0, axis_index_groups=Z_GROUPS)  12.2 us
    all_to_all x1, blocking collectives, body(): terms = lax.all_to_all(terms, 'head', 0, 0)  11.1 us
    all_to_all x1, waiting for transfers between devices, body(): part = lax.all_to_all(part, 'seq', 0, 0, axis_index_groups=Z_GROUPS)  8.07 us
    ppermute x6, starting transfers between devices, permute_y(): lax.ppermute(v, 'head', [(i, (i + 2 * k) % (2 * NY)) for i in range(2 * N...  8.06 us
    ppermute x9, waiting for transfers between devices, permute_x(): lax.ppermute(v, 'seq', [(i, i // NX * NX + (i % NX + k) % NX) for i in ra...  7.11 us
  transfers between devices with their start and end apart: 18, of which 9 were waited for; matrix products, arithmetic and copies ran while one was open for 1% of the time, Pallas kernels for 13%

profile of v1, /device:TPU:1, one launch (start us, length us, event | category | flops | bytes accessed | tf_op | source)
XLA Modules:
  0.0 190.7 jit_solution(5448019073957713007)
XLA Ops:
  0.0 2.1 %collective-permute-start.3 = (bf16[192,1536]{1,0:T(8,128)(2,1)}, bf16[192,1536]{1,0:T(8,128)(2,1)S(1)}, u32[]{:S(2)}, u32[]{:S(2)}) collective-permute-start(bf16[192,1536]{1,0:T(8,128)(2,1)} %w0), channel_id=1, source_target_pairs={{0,2},{1,3},{2,4},{3,5},{4,6},{5,7},{6,0},{7,1},{8,10},{9,11},{10,... | collective-permute-start | bytes 1769480 | tf_op jit(solution)/shard_map/ppermute | solution.py:427
  2.1 1.4 collective-permute-start.4
  3.6 16.8 %encode.1 = (bf16[2,2,112,256]{3,2,1,0:T(8,128)(2,1)}, bf16[2,2,112,256]{3,2,1,0:T(8,128)(2,1)}, bf16[2,2,112,256]{3,2,1,0:T(8,128)(2,1)}, bf16[2048,192]{1,0:T(8,128)(2,1)}, bf16[2,112,2048]{2,1,0:T(8,128)(2,1)}) custom-call(s32[1]{0:T(128)} %bitcast.where, bf16[2048,512]{1,0:T(8,128)(2,1)} %points.1, bf16[8,4,64,1536]{3,2,1,0:T(8,128)(2,1)} %bitcast.17, ...), custom_call_target="tpu_custom_call" | custom-call | flops 16000000000 | bytes 10000000 | tf_op jit(solution)/shard_map/encode/pallas_call | solution.py:264
  20.4 2.8 %collective-permute-start = (bf16[2,2,112,256]{3,2,1,0:T(8,128)(2,1)}, bf16[2,2,112,256]{3,2,1,0:T(8,128)(2,1)S(1)}, u32[]{:S(2)}, u32[]{:S(2)}) collective-permute-start(bf16[2,2,112,256]{3,2,1,0:T(8,128)(2,1)} %get-tuple-element.25), channel_id=1, source_target_pairs={{0,16},{8,24},{16,0},{24,8},{32,48},{40,56},{48,32},{56,40},{64,80... | collective-permute-start | bytes 688136 | tf_op jit(solution)/shard_map/ppermute | solution.py:421
  23.2 62.3 %collective-permute-start.1 = (bf16[2,2,112,256]{3,2,1,0:T(8,128)(2,1)}, bf16[2,2,112,256]{3,2,1,0:T(8,128)(2,1)S(1)}, u32[]{:S(2)}, u32[]{:S(2)}) collective-permute-start(bf16[2,2,112,256]{3,2,1,0:T(8,128)(2,1)} %get-tuple-element.26), channel_id=1, source_target_pairs={{0,8},{8,16},{16,24},{24,0},{32,40},{40,48},{48,56},{56,32},{64,72... | collective-permute-start | bytes 688136 | tf_op jit(solution)/shard_map/ppermute | solution.py:421
  85.4 0.5 collective-permute-start.2
  86.0 6.8 %own.1.a = bf16[2,2,112,256]{3,2,1,0:T(8,128)(2,1)} custom-call(s32[1]{0:T(128)} %bitcast.where, bf16[8,4,64,1536]{3,2,1,0:T(8,128)(2,1)} %bitcast.18, f32[12,128]{1,0:T(8,128)} %bitcast.24, bf16[192,1536]{1,0:T(8,128)(2,1)} %bitcast.20, bf16[2048,192]{1,0:T(8,128)(2,1)} %get-tuple-element.23.keys_in, bf16[2,112,2048]{2,1,0:T(8,128)(2,1)} %get-tuple-element.24.values_in), custom_call_target="tpu_custom_call" | custom-call | flops 4000000000 | bytes 5000000 | tf_op jit(solution)/shard_map/own/pallas_call | solution.py:295
  92.8 0.0 copy-start
  92.8 0.0 collective-permute-done.b
  92.8 0.0 collective-permute-done.1.c
  92.8 2.9 %collective-permute-done.2.d = bf16[2,2,112,256]{3,2,1,0:T(8,128)(2,1)S(1)} collective-permute-done((bf16[2,2,112,256]{3,2,1,0:T(8,128)(2,1)}, bf16[2,2,112,256]{3,2,1,0:T(8,128)(2,1)S(1)}, u32[]{:S(2)}, u32[]{:S(2)}) %collective-permute-start.2) | collective-permute-done | bytes 229408 | tf_op jit(solution)/shard_map/ppermute | solution.py:421
  95.7 0.0 copy-start.6
  95.7 0.9 copy-done.6
  96.7 1.0 combine.1
  97.7 0.0 copy-done
  97.7 1.6 collective-permute-start.5
  99.3 27.9 %all-to-all-start = ((bf16[8,112,128]{2,1,0:T(8,128)(2,1)}), bf16[8,112,128]{2,1,0:T(8,128)(2,1)S(1)}, u32[]{:S(2)}, u32[]{:S(2)}) async-start(bf16[8,112,128]{2,1,0:T(8,128)(2,1)} %combine.1), calls=%async_computation | async-start | bytes 458752 | tf_op jit(solution)/shard_map/all_to_all | solution.py:473
  127.2 0.9 constant_dynamic-slice_fusion.1.latents
  128.1 0.0 collective-permute-done.3.w1
  128.1 0.0 collective-permute-done.4.w2
  128.1 8.1 %all-to-all-done.part = bf16[8,112,128]{2,1,0:T(8,128)(2,1)S(1)} async-done(((bf16[8,112,128]{2,1,0:T(8,128)(2,1)}), bf16[8,112,128]{2,1,0:T(8,128)(2,1)S(1)}, u32[]{:S(2)}, u32[]{:S(2)}) %all-to-all-start) | async-done | bytes 229408 | tf_op jit(solution)/shard_map/all_to_all | solution.py:473
  136.2 0.0 collective-permute-done.5.w3
  136.2 0.2 finish.1.a0
  136.4 0.0 copy-start.1
  136.4 0.0 copy-start.2
  136.5 0.0 copy-start.3
  136.5 0.0 copy-start.5
  136.5 0.5 collective-permute-start.6
  137.0 2.3 %collective-permute-start.7 = (bf16[64,192]{1,0:T(8,128)(2,1)S(1)}, bf16[64,192]{1,0:T(8,128)(2,1)S(1)}, u32[]{:S(2)}, u32[]{:S(2)}) collective-permute-start(bf16[64,192]{1,0:T(8,128)(2,1)S(1)} %finish.1.a0), channel_id=1, source_target_pairs={{0,6},{1,7},{2,0},{3,1},{4,2},{5,3},{6,4},{7,5},{8,14},{9,15},{10,... | collective-permute-start | bytes 73736 | tf_op jit(solution)/shard_map/ppermute | solution.py:427
  139.2 0.1 collective-permute-start.8
  139.4 1.2 collective-permute-done.6.a1
  140.5 0.0 collective-permute-done.7.a2
  140.5 3.0 %collective-permute-done.8.a3 = bf16[64,192]{1,0:T(8,128)(2,1)S(1)} collective-permute-done((bf16[64,192]{1,0:T(8,128)(2,1)S(1)}, bf16[64,192]{1,0:T(8,128)(2,1)S(1)}, u32[]{:S(2)}, u32[]{:S(2)}) %collective-permute-start.8) | collective-permute-done | bytes 24608 | tf_op jit(solution)/shard_map/ppermute | solution.py:427
  143.5 0.5 near.1.own
  144.1 5.5 %collective-permute-start.9 = (f32[64,1536]{1,0:T(8,128)S(1)}, f32[64,1536]{1,0:T(8,128)S(1)}, u32[]{:S(2)}, u32[]{:S(2)}) collective-permute-start(f32[64,1536]{1,0:T(8,128)S(1)} %near.1.own), channel_id=1, source_target_pairs={{0,1},{1,0},{2,3},{3,2},{4,5},{5,4},{6,7},{7,6},{8,9},{9,8},{10,11... | collective-permute-start | bytes 1179656 | tf_op jit(solution)/shard_map/ppermute | solution.py:431
  149.6 1.3 collective-permute-done.9.other
  150.9 0.0 copy-done.1
  150.9 0.0 copy-done.2
  150.9 0.0 copy-done.3
  150.9 0.0 copy-done.5
  150.9 1.7 middle.1
  152.6 3.5 %all-to-all-start.1 = ((bf16[8,64,384]{2,1,0:T(8,128)(2,1)}), bf16[8,64,384]{2,1,0:T(8,128)(2,1)S(1)}, u32[]{:S(2)}, u32[]{:S(2)}) async-start(bf16[8,64,384]{2,1,0:T(8,128)(2,1)} %get-tuple-element.36), calls=%async_computation.1 | async-start | bytes 786432 | tf_op jit(solution)/shard_map/all_to_all | solution.py:490
  156.1 0.1 collective-permute-start.10
  156.2 2.7 %collective-permute-start.11 = (bf16[64,192]{1,0:T(8,128)(2,1)S(1)}, bf16[64,192]{1,0:T(8,128)(2,1)S(1)}, u32[]{:S(2)}, u32[]{:S(2)}) collective-permute-start(bf16[64,192]{1,0:T(8,128)(2,1)S(1)} %get-tuple-element.40.q0), channel_id=1, source_target_pairs={{0,24},{8,0},{16,8},{24,16},{32,56},{40,32},{48,40},{56,48},{64,88... | collective-permute-start | bytes 73736 | tf_op jit(solution)/shard_map/ppermute | solution.py:421
  158.8 0.0 collective-permute-start.12
  158.8 0.1 constant_dynamic-slice_fusion.mid
  158.9 12.2 %all-to-all-done.1 = bf16[8,64,384]{2,1,0:T(8,128)(2,1)S(1)} async-done(((bf16[8,64,384]{2,1,0:T(8,128)(2,1)}), bf16[8,64,384]{2,1,0:T(8,128)(2,1)S(1)}, u32[]{:S(2)}, u32[]{:S(2)}) %all-to-all-start.1) | async-done | bytes 393248 | tf_op jit(solution)/shard_map/all_to_all | solution.py:490
  171.2 0.0 collective-permute-done.10.q1
  171.2 0.0 collective-permute-done.11.q2
  171.2 0.0 collective-permute-done.12.q3
  171.2 0.0 copy-start.4
  171.2 1.5 self_part.1
  172.7 0.1 collective-permute-start.13
  172.8 1.5 collective-permute-start.14
  174.2 0.0 collective-permute-start.15
  174.2 1.3 collective-permute-done.13.p1
  175.5 1.3 collective-permute-done.14.p2
  176.8 1.7 collective-permute-done.15.p3
  178.5 0.0 copy-done.4
  178.5 0.5 output.1
  178.9 11.1 %all_to_all.15.terms = bf16[8,64,192]{2,1,0:T(8,128)(2,1)S(1)} all-to-all(bf16[8,64,192]{2,1,0:T(8,128)(2,1)S(1)} %output.1), channel_id=1, replica_groups=mesh['seq'=32,'head'=8] {'head'}, dimensions={0} | all-to-all | bytes 393216 | tf_op jit(solution)/shard_map/all_to_all | solution.py:502
  190.0 0.7 add.14
  (1 shorter events, 0.0 us)
Async XLA Ops:
  0.0 128.1 %collective-permute-start.3 = (bf16[192,1536]{1,0:T(8,128)(2,1)}, bf16[192,1536]{1,0:T(8,128)(2,1)S(1)}, u32[]{:S(2)}, u32[]{:S(2)}) collective-permute-start(bf16[192,1536]{1,0:T(8,128)(2,1)} %w0), channel_id=1, source_target_pairs={{0,2},{1,3},{2,4},{3,5},{4,6},{5,7},{6,0},{7,1},{8,10},{9,11},{10,... | collective-permute-start | bytes 1769480 | tf_op jit(solution)/shard_map/ppermute | solution.py:427
  2.1 126.0 %collective-permute-start.4 = (bf16[192,1536]{1,0:T(8,128)(2,1)}, bf16[192,1536]{1,0:T(8,128)(2,1)S(1)}, u32[]{:S(2)}, u32[]{:S(2)}) collective-permute-start(bf16[192,1536]{1,0:T(8,128)(2,1)} %w0), channel_id=1, source_target_pairs={{0,6},{1,7},{2,0},{3,1},{4,2},{5,3},{6,4},{7,5},{8,14},{9,15},{10,... | collective-permute-start | bytes 1769480 | tf_op jit(solution)/shard_map/ppermute | solution.py:427
  20.4 72.5 %collective-permute-start = (bf16[2,2,112,256]{3,2,1,0:T(8,128)(2,1)}, bf16[2,2,112,256]{3,2,1,0:T(8,128)(2,1)S(1)}, u32[]{:S(2)}, u32[]{:S(2)}) collective-permute-start(bf16[2,2,112,256]{3,2,1,0:T(8,128)(2,1)} %get-tuple-element.25), channel_id=1, source_target_pairs={{0,16},{8,24},{16,0},{24,8},{32,48},{40,56},{48,32},{56,40},{64,80... | collective-permute-start | bytes 688136 | tf_op jit(solution)/shard_map/ppermute | solution.py:421
  23.2 69.6 %collective-permute-start.1 = (bf16[2,2,112,256]{3,2,1,0:T(8,128)(2,1)}, bf16[2,2,112,256]{3,2,1,0:T(8,128)(2,1)S(1)}, u32[]{:S(2)}, u32[]{:S(2)}) collective-permute-start(bf16[2,2,112,256]{3,2,1,0:T(8,128)(2,1)} %get-tuple-element.26), channel_id=1, source_target_pairs={{0,8},{8,16},{16,24},{24,0},{32,40},{40,48},{48,56},{56,32},{64,72... | collective-permute-start | bytes 688136 | tf_op jit(solution)/shard_map/ppermute | solution.py:421
  85.4 10.3 %collective-permute-start.2 = (bf16[2,2,112,256]{3,2,1,0:T(8,128)(2,1)}, bf16[2,2,112,256]{3,2,1,0:T(8,128)(2,1)S(1)}, u32[]{:S(2)}, u32[]{:S(2)}) collective-permute-start(bf16[2,2,112,256]{3,2,1,0:T(8,128)(2,1)} %get-tuple-element.27), channel_id=1, source_target_pairs={{0,24},{8,0},{16,8},{24,16},{32,56},{40,32},{48,40},{56,48},{64,88... | collective-permute-start | bytes 688136 | tf_op jit(solution)/shard_map/ppermute | solution.py:421
  92.8 4.9 %copy-start = (bf16[192,1536]{1,0:T(8,128)(2,1)S(1)}, bf16[192,1536]{1,0:T(8,128)(2,1)}, u32[]{:S(2)}) copy-start(bf16[192,1536]{1,0:T(8,128)(2,1)} %w0) | copy-start | bytes 1769476
  95.7 0.9 copy-start.6
  97.7 38.5 %collective-permute-start.5 = (bf16[192,1536]{1,0:T(8,128)(2,1)S(1)}, bf16[192,1536]{1,0:T(8,128)(2,1)S(1)}, u32[]{:S(2)}, u32[]{:S(2)}) collective-permute-start(bf16[192,1536]{1,0:T(8,128)(2,1)S(1)} %copy-done), channel_id=1, source_target_pairs={{0,4},{1,5},{2,6},{3,7},{4,0},{5,1},{6,2},{7,3},{8,12},{9,13},{10,... | collective-permute-start | bytes 1769480 | tf_op jit(solution)/shard_map/ppermute | solution.py:427
  99.3 36.9 %all-to-all-start = ((bf16[8,112,128]{2,1,0:T(8,128)(2,1)}), bf16[8,112,128]{2,1,0:T(8,128)(2,1)S(1)}, u32[]{:S(2)}, u32[]{:S(2)}) async-start(bf16[8,112,128]{2,1,0:T(8,128)(2,1)} %combine.1), calls=%async_computation | async-start | bytes 458752 | tf_op jit(solution)/shard_map/all_to_all | solution.py:473
  136.4 14.5 %copy-start.1 = (bf16[1536,192]{0,1:T(8,128)(2,1)S(1)}, bf16[1536,192]{0,1:T(8,128)(2,1)}, u32[]{:S(2)}) copy-start(bf16[1536,192]{0,1:T(8,128)(2,1)} %param.22) | copy-start | bytes 1769476
  136.4 14.5 %copy-start.2 = (bf16[1536,192]{0,1:T(8,128)(2,1)S(1)}, bf16[1536,192]{0,1:T(8,128)(2,1)}, u32[]{:S(2)}) copy-start(bf16[1536,192]{0,1:T(8,128)(2,1)} %param.23) | copy-start | bytes 1769476
  136.5 14.5 %copy-start.3 = (bf16[1536,192]{0,1:T(8,128)(2,1)S(1)}, bf16[1536,192]{0,1:T(8,128)(2,1)}, u32[]{:S(2)}) copy-start(bf16[1536,192]{0,1:T(8,128)(2,1)} %param.24) | copy-start | bytes 1769476
  136.5 14.4 %copy-start.5 = (f32[1536]{0:T(1024)S(1)}, f32[1536]{0:T(1024)}, u32[]{:S(2)}) copy-start(f32[1536]{0:T(1024)} %param.17) | copy-start | bytes 18436
  136.5 4.1 %collective-permute-start.6 = (bf16[64,192]{1,0:T(8,128)(2,1)S(1)}, bf16[64,192]{1,0:T(8,128)(2,1)S(1)}, u32[]{:S(2)}, u32[]{:S(2)}) collective-permute-start(bf16[64,192]{1,0:T(8,128)(2,1)S(1)} %finish.1.a0), channel_id=1, source_target_pairs={{0,2},{1,3},{2,4},{3,5},{4,6},{5,7},{6,0},{7,1},{8,10},{9,11},{10,... | collective-permute-start | bytes 73736 | tf_op jit(solution)/shard_map/ppermute | solution.py:427
  137.0 3.6 %collective-permute-start.7 = (bf16[64,192]{1,0:T(8,128)(2,1)S(1)}, bf16[64,192]{1,0:T(8,128)(2,1)S(1)}, u32[]{:S(2)}, u32[]{:S(2)}) collective-permute-start(bf16[64,192]{1,0:T(8,128)(2,1)S(1)} %finish.1.a0), channel_id=1, source_target_pairs={{0,6},{1,7},{2,0},{3,1},{4,2},{5,3},{6,4},{7,5},{8,14},{9,15},{10,... | collective-permute-start | bytes 73736 | tf_op jit(solution)/shard_map/ppermute | solution.py:427
  139.2 4.3 %collective-permute-start.8 = (bf16[64,192]{1,0:T(8,128)(2,1)S(1)}, bf16[64,192]{1,0:T(8,128)(2,1)S(1)}, u32[]{:S(2)}, u32[]{:S(2)}) collective-permute-start(bf16[64,192]{1,0:T(8,128)(2,1)S(1)} %finish.1.a0), channel_id=1, source_target_pairs={{0,4},{1,5},{2,6},{3,7},{4,0},{5,1},{6,2},{7,3},{8,12},{9,13},{10,... | collective-permute-start | bytes 73736 | tf_op jit(solution)/shard_map/ppermute | solution.py:427
  144.1 6.9 %collective-permute-start.9 = (f32[64,1536]{1,0:T(8,128)S(1)}, f32[64,1536]{1,0:T(8,128)S(1)}, u32[]{:S(2)}, u32[]{:S(2)}) collective-permute-start(f32[64,1536]{1,0:T(8,128)S(1)} %near.1.own), channel_id=1, source_target_pairs={{0,1},{1,0},{2,3},{3,2},{4,5},{5,4},{6,7},{7,6},{8,9},{9,8},{10,11... | collective-permute-start | bytes 1179656 | tf_op jit(solution)/shard_map/ppermute | solution.py:431
  152.6 18.5 %all-to-all-start.1 = ((bf16[8,64,384]{2,1,0:T(8,128)(2,1)}), bf16[8,64,384]{2,1,0:T(8,128)(2,1)S(1)}, u32[]{:S(2)}, u32[]{:S(2)}) async-start(bf16[8,64,384]{2,1,0:T(8,128)(2,1)} %get-tuple-element.36), calls=%async_computation.1 | async-start | bytes 786432 | tf_op jit(solution)/shard_map/all_to_all | solution.py:490
  156.1 15.1 %collective-permute-start.10 = (bf16[64,192]{1,0:T(8,128)(2,1)S(1)}, bf16[64,192]{1,0:T(8,128)(2,1)S(1)}, u32[]{:S(2)}, u32[]{:S(2)}) collective-permute-start(bf16[64,192]{1,0:T(8,128)(2,1)S(1)} %get-tuple-element.40.q0), channel_id=1, source_target_pairs={{0,8},{8,16},{16,24},{24,0},{32,40},{40,48},{48,56},{56,32},{64,72... | collective-permute-start | bytes 73736 | tf_op jit(solution)/shard_map/ppermute | solution.py:421
  156.2 15.0 %collective-permute-start.11 = (bf16[64,192]{1,0:T(8,128)(2,1)S(1)}, bf16[64,192]{1,0:T(8,128)(2,1)S(1)}, u32[]{:S(2)}, u32[]{:S(2)}) collective-permute-start(bf16[64,192]{1,0:T(8,128)(2,1)S(1)} %get-tuple-element.40.q0), channel_id=1, source_target_pairs={{0,24},{8,0},{16,8},{24,16},{32,56},{40,32},{48,40},{56,48},{64,88... | collective-permute-start | bytes 73736 | tf_op jit(solution)/shard_map/ppermute | solution.py:421
  158.8 12.3 %collective-permute-start.12 = (bf16[64,192]{1,0:T(8,128)(2,1)S(1)}, bf16[64,192]{1,0:T(8,128)(2,1)S(1)}, u32[]{:S(2)}, u32[]{:S(2)}) collective-permute-start(bf16[64,192]{1,0:T(8,128)(2,1)S(1)} %get-tuple-element.40.q0), channel_id=1, source_target_pairs={{0,16},{8,24},{16,0},{24,8},{32,48},{40,56},{48,32},{56,40},{64,80... | collective-permute-start | bytes 73736 | tf_op jit(solution)/shard_map/ppermute | solution.py:421
  171.2 7.3 %copy-start.4 = (bf16[192,1536]{1,0:T(8,128)(2,1)S(1)}, bf16[192,1536]{1,0:T(8,128)(2,1)}, u32[]{:S(2)}) copy-start(bf16[192,1536]{1,0:T(8,128)(2,1)} %w.1) | copy-start | bytes 1769476
  172.7 2.8 %collective-permute-start.13 = (bf16[1,112,128]{2,1,0:T(8,128)(2,1)S(1)}, bf16[1,112,128]{2,1,0:T(8,128)(2,1)S(1)}, u32[]{:S(2)}, u32[]{:S(2)}) collective-permute-start(bf16[1,112,128]{2,1,0:T(8,128)(2,1)S(1)} %get-tuple-element.43), channel_id=1, source_target_pairs={{0,24},{8,0},{16,8},{24,16},{32,56},{40,32},{48,40},{56,48},{64,88... | collective-permute-start | bytes 86024 | tf_op jit(solution)/shard_map/ppermute | solution.py:421
  172.8 4.0 %collective-permute-start.14 = (bf16[1,112,128]{2,1,0:T(8,128)(2,1)S(1)}, bf16[1,112,128]{2,1,0:T(8,128)(2,1)S(1)}, u32[]{:S(2)}, u32[]{:S(2)}) collective-permute-start(bf16[1,112,128]{2,1,0:T(8,128)(2,1)S(1)} %get-tuple-element.42), channel_id=1, source_target_pairs={{0,8},{8,16},{16,24},{24,0},{32,40},{40,48},{48,56},{56,32},{64,72... | collective-permute-start | bytes 86024 | tf_op jit(solution)/shard_map/ppermute | solution.py:421
  174.2 4.2 %collective-permute-start.15 = (bf16[1,112,128]{2,1,0:T(8,128)(2,1)S(1)}, bf16[1,112,128]{2,1,0:T(8,128)(2,1)S(1)}, u32[]{:S(2)}, u32[]{:S(2)}) collective-permute-start(bf16[1,112,128]{2,1,0:T(8,128)(2,1)S(1)} %get-tuple-element.41), channel_id=1, source_target_pairs={{0,16},{8,24},{16,0},{24,8},{32,48},{40,56},{48,32},{56,40},{64,80... | collective-permute-start | bytes 86024 | tf_op jit(solution)/shard_map/ppermute | solution.py:421

commit v2 on v1

--- a/solution.py
+++ b/solution.py
@@ -432,7 +432,8 @@
 
 
 def gather_y(v):
-    return [v] + [permute_y(v, k) for k in SHIFTS]
+    got = {k: permute_y(v, k) for k in FOREIGN}
+    return [v] + [got[k] for k in SHIFTS]
 
 
 def body(

time: 190 us -> 191 us (level)
  Pallas kernels: 29.7 us -> 112 us
  starting transfers between devices: 115 us -> 34.4 us
  waiting for transfers between devices: 32.9 us -> 30.2 us
    pallas_call x1, Pallas kernels: 16.8 us -> 78.7 us  [encode_call(): pl.pallas_call(encode_kernel, out_shape=(part, part, part, keys, values_t...]
    ppermute x9, starting transfers between devices: 69.9 us -> 9.79 us  [permute_x(): lax.ppermute(v, 'seq', [(i, i // NX * NX + (i % NX + k) % NX) for i in ra...]
    pallas_call x1, Pallas kernels: 6.83 us -> 27.5 us  [own_call(): pl.pallas_call(own_kernel, out_shape=jax.ShapeDtypeStruct((nz * rows // L...]
    all_to_all x1, starting transfers between devices: 27.9 us -> 8.2 us  [body(): part = lax.all_to_all(part, 'seq', 0, 0, axis_index_groups=Z_GROUPS)]
    ppermute x9, waiting for transfers between devices: 7.11 us -> 4.24 us  [permute_x(): lax.ppermute(v, 'seq', [(i, i // NX * NX + (i % NX + k) % NX) for i in ra...]
  transfers between devices with their start and end apart: 18 -> 18, of which waited for: 9 -> 8; matrix products, arithmetic and copies ran while one was open for 1% -> 1% of each run, Pallas kernels for 13% -> 56%
where the time goes in v2:
time: 191 us; the launch traced here: 190 us
  Pallas kernels  112 us (59%)
  starting transfers between devices  34.4 us (18%)
  waiting for transfers between devices  30.2 us (16%)
  blocking collectives  11.1 us (6%)
  local copies, waits for them, and re-layouts  2.06 us (1%)
    pallas_call x1, Pallas kernels, encode_call(): pl.pallas_call(encode_kernel, out_shape=(part, part, part, keys, values_t...  78.7 us
    pallas_call x1, Pallas kernels, own_call(): pl.pallas_call(own_kernel, out_shape=jax.ShapeDtypeStruct((nz * rows // L...  27.5 us
    all_to_all x1, waiting for transfers between devices, body(): kv = lax.all_to_all(kv, 'seq', 0, 0, axis_index_groups=Z_GROUPS)  12.2 us
    all_to_all x1, blocking collectives, body(): terms = lax.all_to_all(terms, 'head', 0, 0)  11.1 us
    ppermute x9, starting transfers between devices, permute_x(): lax.ppermute(v, 'seq', [(i, i // NX * NX + (i % NX + k) % NX) for i in ra...  9.79 us
    all_to_all x1, starting transfers between devices, body(): part = lax.all_to_all(part, 'seq', 0, 0, axis_index_groups=Z_GROUPS)  8.2 us
    all_to_all x1, waiting for transfers between devices, body(): part = lax.all_to_all(part, 'seq', 0, 0, axis_index_groups=Z_GROUPS)  8.12 us
    ppermute x6, starting transfers between devices, permute_y(): lax.ppermute(v, 'head', [(i, (i + 2 * k) % (2 * NY)) for i in range(2 * N...  7.96 us
  transfers between devices with their start and end apart: 18, of which 8 were waited for; matrix products, arithmetic and copies ran while one was open for 1% of the time, Pallas kernels for 56%

profile of v2, /device:TPU:1, one launch (start us, length us, event | category | flops | bytes accessed | tf_op | source)
XLA Modules:
  0.0 190.3 jit_solution(5448019073957713007)
XLA Ops:
  0.0 2.1 %collective-permute-start.3 = (bf16[192,1536]{1,0:T(8,128)(2,1)}, bf16[192,1536]{1,0:T(8,128)(2,1)S(1)}, u32[]{:S(2)}, u32[]{:S(2)}) collective-permute-start(bf16[192,1536]{1,0:T(8,128)(2,1)} %w0), channel_id=1, source_target_pairs={{0,2},{1,3},{2,4},{3,5},{4,6},{5,7},{6,0},{7,1},{8,10},{9,11},{10,... | collective-permute-start | bytes 1769480 | tf_op jit(solution)/shard_map/ppermute | solution.py:427
  2.1 1.4 collective-permute-start.4
  3.6 78.7 %encode.1 = (bf16[2,2,112,256]{3,2,1,0:T(8,128)(2,1)}, bf16[2,2,112,256]{3,2,1,0:T(8,128)(2,1)}, bf16[2,2,112,256]{3,2,1,0:T(8,128)(2,1)}, bf16[2048,192]{1,0:T(8,128)(2,1)}, bf16[2,112,2048]{2,1,0:T(8,128)(2,1)}) custom-call(s32[1]{0:T(128)} %bitcast.where, bf16[2048,512]{1,0:T(8,128)(2,1)} %points.1, bf16[8,4,64,1536]{3,2,1,0:T(8,128)(2,1)} %bitcast.17, ...), custom_call_target="tpu_custom_call" | custom-call | flops 16000000000 | bytes 10000000 | tf_op jit(solution)/shard_map/encode/pallas_call | solution.py:264
  82.3 2.8 %collective-permute-start = (bf16[2,2,112,256]{3,2,1,0:T(8,128)(2,1)}, bf16[2,2,112,256]{3,2,1,0:T(8,128)(2,1)S(1)}, u32[]{:S(2)}, u32[]{:S(2)}) collective-permute-start(bf16[2,2,112,256]{3,2,1,0:T(8,128)(2,1)} %get-tuple-element.25), channel_id=1, source_target_pairs={{0,16},{8,24},{16,0},{24,8},{32,48},{40,56},{48,32},{56,40},{64,80... | collective-permute-start | bytes 688136 | tf_op jit(solution)/shard_map/ppermute | solution.py:421
  85.1 0.0 collective-permute-start.1
  85.1 2.7 %collective-permute-start.2 = (bf16[2,2,112,256]{3,2,1,0:T(8,128)(2,1)}, bf16[2,2,112,256]{3,2,1,0:T(8,128)(2,1)S(1)}, u32[]{:S(2)}, u32[]{:S(2)}) collective-permute-start(bf16[2,2,112,256]{3,2,1,0:T(8,128)(2,1)} %get-tuple-element.27), channel_id=1, source_target_pairs={{0,24},{8,0},{16,8},{24,16},{32,56},{40,32},{48,40},{56,48},{64,88... | collective-permute-start | bytes 688136 | tf_op jit(solution)/shard_map/ppermute | solution.py:421
  87.8 27.5 %own.1.a = bf16[2,2,112,256]{3,2,1,0:T(8,128)(2,1)} custom-call(s32[1]{0:T(128)} %bitcast.where, bf16[8,4,64,1536]{3,2,1,0:T(8,128)(2,1)} %bitcast.18, f32[12,128]{1,0:T(8,128)} %bitcast.24, bf16[192,1536]{1,0:T(8,128)(2,1)} %bitcast.20, bf16[2048,192]{1,0:T(8,128)(2,1)} %get-tuple-element.23.keys_in, bf16[2,112,2048]{2,1,0:T(8,128)(2,1)} %get-tuple-element.24.values_in), custom_call_target="tpu_custom_call" | custom-call | flops 4000000000 | bytes 5000000 | tf_op jit(solution)/shard_map/own/pallas_call | solution.py:295
  115.3 0.0 copy-start
  115.3 0.0 collective-permute-done.b
  115.3 0.0 collective-permute-done.1.c
  115.3 0.0 collective-permute-done.2.d
  115.3 0.0 copy-start.6
  115.3 1.0 copy-done.6
  116.3 1.0 combine.1
  117.3 0.0 copy-done
  117.3 1.6 collective-permute-start.5
  119.0 8.2 %all-to-all-start = ((bf16[8,112,128]{2,1,0:T(8,128)(2,1)}), bf16[8,112,128]{2,1,0:T(8,128)(2,1)S(1)}, u32[]{:S(2)}, u32[]{:S(2)}) async-start(bf16[8,112,128]{2,1,0:T(8,128)(2,1)} %combine.1), calls=%async_computation | async-start | bytes 458752 | tf_op jit(solution)/shard_map/all_to_all | solution.py:474
  127.2 0.9 constant_dynamic-slice_fusion.1.latents
  128.1 0.0 collective-permute-done.3.w1
  128.1 0.0 collective-permute-done.4.w2
  128.1 8.1 %all-to-all-done.part = bf16[8,112,128]{2,1,0:T(8,128)(2,1)S(1)} async-done(((bf16[8,112,128]{2,1,0:T(8,128)(2,1)}), bf16[8,112,128]{2,1,0:T(8,128)(2,1)S(1)}, u32[]{:S(2)}, u32[]{:S(2)}) %all-to-all-start) | async-done | bytes 229408 | tf_op jit(solution)/shard_map/all_to_all | solution.py:474
  136.3 0.0 collective-permute-done.5.w3
  136.3 0.2 finish.1.a0
  136.5 0.0 copy-start.1
  136.5 0.0 copy-start.2
  136.5 0.0 copy-start.3
  136.5 0.0 copy-start.5
  136.5 0.1 collective-permute-start.6
  136.6 2.7 %collective-permute-start.7 = (bf16[64,192]{1,0:T(8,128)(2,1)S(1)}, bf16[64,192]{1,0:T(8,128)(2,1)S(1)}, u32[]{:S(2)}, u32[]{:S(2)}) collective-permute-start(bf16[64,192]{1,0:T(8,128)(2,1)S(1)} %finish.1.a0), channel_id=1, source_target_pairs={{0,6},{1,7},{2,0},{3,1},{4,2},{5,3},{6,4},{7,5},{8,14},{9,15},{10,... | collective-permute-start | bytes 73736 | tf_op jit(solution)/shard_map/ppermute | solution.py:427
  139.3 0.0 collective-permute-start.8
  139.3 1.3 collective-permute-done.6.a1
  140.6 0.0 collective-permute-done.7.a2
  140.6 3.0 %collective-permute-done.8.a3 = bf16[64,192]{1,0:T(8,128)(2,1)S(1)} collective-permute-done((bf16[64,192]{1,0:T(8,128)(2,1)S(1)}, bf16[64,192]{1,0:T(8,128)(2,1)S(1)}, u32[]{:S(2)}, u32[]{:S(2)}) %collective-permute-start.8) | collective-permute-done | bytes 24608 | tf_op jit(solution)/shard_map/ppermute | solution.py:427
  143.6 0.5 near.1.own
  144.1 5.0 %collective-permute-start.9 = (f32[64,1536]{1,0:T(8,128)S(1)}, f32[64,1536]{1,0:T(8,128)S(1)}, u32[]{:S(2)}, u32[]{:S(2)}) collective-permute-start(f32[64,1536]{1,0:T(8,128)S(1)} %near.1.own), channel_id=1, source_target_pairs={{0,1},{1,0},{2,3},{3,2},{4,5},{5,4},{6,7},{7,6},{8,9},{9,8},{10,11... | collective-permute-start | bytes 1179656 | tf_op jit(solution)/shard_map/ppermute | solution.py:431
  149.1 1.3 collective-permute-done.9.other
  150.5 0.0 copy-done.1
  150.5 0.0 copy-done.2
  150.5 0.0 copy-done.3
  150.5 0.0 copy-done.5
  150.5 1.7 middle.1
  152.2 3.5 %all-to-all-start.1 = ((bf16[8,64,384]{2,1,0:T(8,128)(2,1)}), bf16[8,64,384]{2,1,0:T(8,128)(2,1)S(1)}, u32[]{:S(2)}, u32[]{:S(2)}) async-start(bf16[8,64,384]{2,1,0:T(8,128)(2,1)} %get-tuple-element.36), calls=%async_computation.1 | async-start | bytes 786432 | tf_op jit(solution)/shard_map/all_to_all | solution.py:491
  155.7 0.1 collective-permute-start.10
  155.7 2.7 %collective-permute-start.11 = (bf16[64,192]{1,0:T(8,128)(2,1)S(1)}, bf16[64,192]{1,0:T(8,128)(2,1)S(1)}, u32[]{:S(2)}, u32[]{:S(2)}) collective-permute-start(bf16[64,192]{1,0:T(8,128)(2,1)S(1)} %get-tuple-element.40.q0), channel_id=1, source_target_pairs={{0,24},{8,0},{16,8},{24,16},{32,56},{40,32},{48,40},{56,48},{64,88... | collective-permute-start | bytes 73736 | tf_op jit(solution)/shard_map/ppermute | solution.py:421
  158.4 0.0 collective-permute-start.12
  158.4 0.1 constant_dynamic-slice_fusion.mid
  158.5 12.2 %all-to-all-done.1 = bf16[8,64,384]{2,1,0:T(8,128)(2,1)S(1)} async-done(((bf16[8,64,384]{2,1,0:T(8,128)(2,1)}), bf16[8,64,384]{2,1,0:T(8,128)(2,1)S(1)}, u32[]{:S(2)}, u32[]{:S(2)}) %all-to-all-start.1) | async-done | bytes 393248 | tf_op jit(solution)/shard_map/all_to_all | solution.py:491
  170.7 0.0 collective-permute-done.10.q1
  170.7 0.0 collective-permute-done.11.q2
  170.7 0.0 collective-permute-done.12.q3
  170.7 0.0 copy-start.4
  170.8 1.5 self_part.1
  172.3 0.2 collective-permute-start.13
  172.4 1.4 collective-permute-start.14
  173.8 0.0 collective-permute-start.15
  173.8 1.3 collective-permute-done.13.p1
  175.1 1.3 collective-permute-done.14.p2
  176.4 1.7 collective-permute-done.15.p3
  178.0 0.0 copy-done.4
  178.0 0.5 output.1
  178.5 11.1 %all_to_all.15.terms = bf16[8,64,192]{2,1,0:T(8,128)(2,1)S(1)} all-to-all(bf16[8,64,192]{2,1,0:T(8,128)(2,1)S(1)} %output.1), channel_id=1, replica_groups=mesh['seq'=32,'head'=8] {'head'}, dimensions={0} | all-to-all | bytes 393216 | tf_op jit(solution)/shard_map/all_to_all | solution.py:503
  189.6 0.7 add.14
  (1 shorter events, 0.0 us)
Async XLA Ops:
  0.0 128.1 %collective-permute-start.3 = (bf16[192,1536]{1,0:T(8,128)(2,1)}, bf16[192,1536]{1,0:T(8,128)(2,1)S(1)}, u32[]{:S(2)}, u32[]{:S(2)}) collective-permute-start(bf16[192,1536]{1,0:T(8,128)(2,1)} %w0), channel_id=1, source_target_pairs={{0,2},{1,3},{2,4},{3,5},{4,6},{5,7},{6,0},{7,1},{8,10},{9,11},{10,... | collective-permute-start | bytes 1769480 | tf_op jit(solution)/shard_map/ppermute | solution.py:427
  2.1 126.0 %collective-permute-start.4 = (bf16[192,1536]{1,0:T(8,128)(2,1)}, bf16[192,1536]{1,0:T(8,128)(2,1)S(1)}, u32[]{:S(2)}, u32[]{:S(2)}) collective-permute-start(bf16[192,1536]{1,0:T(8,128)(2,1)} %w0), channel_id=1, source_target_pairs={{0,6},{1,7},{2,0},{3,1},{4,2},{5,3},{6,4},{7,5},{8,14},{9,15},{10,... | collective-permute-start | bytes 1769480 | tf_op jit(solution)/shard_map/ppermute | solution.py:427
  82.3 33.0 %collective-permute-start = (bf16[2,2,112,256]{3,2,1,0:T(8,128)(2,1)}, bf16[2,2,112,256]{3,2,1,0:T(8,128)(2,1)S(1)}, u32[]{:S(2)}, u32[]{:S(2)}) collective-permute-start(bf16[2,2,112,256]{3,2,1,0:T(8,128)(2,1)} %get-tuple-element.25), channel_id=1, source_target_pairs={{0,16},{8,24},{16,0},{24,8},{32,48},{40,56},{48,32},{56,40},{64,80... | collective-permute-start | bytes 688136 | tf_op jit(solution)/shard_map/ppermute | solution.py:421
  85.1 30.2 %collective-permute-start.1 = (bf16[2,2,112,256]{3,2,1,0:T(8,128)(2,1)}, bf16[2,2,112,256]{3,2,1,0:T(8,128)(2,1)S(1)}, u32[]{:S(2)}, u32[]{:S(2)}) collective-permute-start(bf16[2,2,112,256]{3,2,1,0:T(8,128)(2,1)} %get-tuple-element.26), channel_id=1, source_target_pairs={{0,8},{8,16},{16,24},{24,0},{32,40},{40,48},{48,56},{56,32},{64,72... | collective-permute-start | bytes 688136 | tf_op jit(solution)/shard_map/ppermute | solution.py:421
  85.1 30.2 %collective-permute-start.2 = (bf16[2,2,112,256]{3,2,1,0:T(8,128)(2,1)}, bf16[2,2,112,256]{3,2,1,0:T(8,128)(2,1)S(1)}, u32[]{:S(2)}, u32[]{:S(2)}) collective-permute-start(bf16[2,2,112,256]{3,2,1,0:T(8,128)(2,1)} %get-tuple-element.27), channel_id=1, source_target_pairs={{0,24},{8,0},{16,8},{24,16},{32,56},{40,32},{48,40},{56,48},{64,88... | collective-permute-start | bytes 688136 | tf_op jit(solution)/shard_map/ppermute | solution.py:421
  115.3 2.1 %copy-start = (bf16[192,1536]{1,0:T(8,128)(2,1)S(1)}, bf16[192,1536]{1,0:T(8,128)(2,1)}, u32[]{:S(2)}) copy-start(bf16[192,1536]{1,0:T(8,128)(2,1)} %w0) | copy-start | bytes 1769476
  115.3 1.0 copy-start.6
  117.3 18.9 %collective-permute-start.5 = (bf16[192,1536]{1,0:T(8,128)(2,1)S(1)}, bf16[192,1536]{1,0:T(8,128)(2,1)S(1)}, u32[]{:S(2)}, u32[]{:S(2)}) collective-permute-start(bf16[192,1536]{1,0:T(8,128)(2,1)S(1)} %copy-done), channel_id=1, source_target_pairs={{0,4},{1,5},{2,6},{3,7},{4,0},{5,1},{6,2},{7,3},{8,12},{9,13},{10,... | collective-permute-start | bytes 1769480 | tf_op jit(solution)/shard_map/ppermute | solution.py:427
  119.0 17.3 %all-to-all-start = ((bf16[8,112,128]{2,1,0:T(8,128)(2,1)}), bf16[8,112,128]{2,1,0:T(8,128)(2,1)S(1)}, u32[]{:S(2)}, u32[]{:S(2)}) async-start(bf16[8,112,128]{2,1,0:T(8,128)(2,1)} %combine.1), calls=%async_computation | async-start | bytes 458752 | tf_op jit(solution)/shard_map/all_to_all | solution.py:474
  136.5 14.0 %copy-start.1 = (bf16[1536,192]{0,1:T(8,128)(2,1)S(1)}, bf16[1536,192]{0,1:T(8,128)(2,1)}, u32[]{:S(2)}) copy-start(bf16[1536,192]{0,1:T(8,128)(2,1)} %param.22) | copy-start | bytes 1769476
  136.5 14.0 %copy-start.2 = (bf16[1536,192]{0,1:T(8,128)(2,1)S(1)}, bf16[1536,192]{0,1:T(8,128)(2,1)}, u32[]{:S(2)}) copy-start(bf16[1536,192]{0,1:T(8,128)(2,1)} %param.23) | copy-start | bytes 1769476
  136.5 14.0 %copy-start.3 = (bf16[1536,192]{0,1:T(8,128)(2,1)S(1)}, bf16[1536,192]{0,1:T(8,128)(2,1)}, u32[]{:S(2)}) copy-start(bf16[1536,192]{0,1:T(8,128)(2,1)} %param.24) | copy-start | bytes 1769476
  136.5 14.0 %copy-start.5 = (f32[1536]{0:T(1024)S(1)}, f32[1536]{0:T(1024)}, u32[]{:S(2)}) copy-start(f32[1536]{0:T(1024)} %param.17) | copy-start | bytes 18436
  136.5 4.1 %collective-permute-start.6 = (bf16[64,192]{1,0:T(8,128)(2,1)S(1)}, bf16[64,192]{1,0:T(8,128)(2,1)S(1)}, u32[]{:S(2)}, u32[]{:S(2)}) collective-permute-start(bf16[64,192]{1,0:T(8,128)(2,1)S(1)} %finish.1.a0), channel_id=1, source_target_pairs={{0,2},{1,3},{2,4},{3,5},{4,6},{5,7},{6,0},{7,1},{8,10},{9,11},{10,... | collective-permute-start | bytes 73736 | tf_op jit(solution)/shard_map/ppermute | solution.py:427
  136.6 4.0 %collective-permute-start.7 = (bf16[64,192]{1,0:T(8,128)(2,1)S(1)}, bf16[64,192]{1,0:T(8,128)(2,1)S(1)}, u32[]{:S(2)}, u32[]{:S(2)}) collective-permute-start(bf16[64,192]{1,0:T(8,128)(2,1)S(1)} %finish.1.a0), channel_id=1, source_target_pairs={{0,6},{1,7},{2,0},{3,1},{4,2},{5,3},{6,4},{7,5},{8,14},{9,15},{10,... | collective-permute-start | bytes 73736 | tf_op jit(solution)/shard_map/ppermute | solution.py:427
  139.3 4.3 %collective-permute-start.8 = (bf16[64,192]{1,0:T(8,128)(2,1)S(1)}, bf16[64,192]{1,0:T(8,128)(2,1)S(1)}, u32[]{:S(2)}, u32[]{:S(2)}) collective-permute-start(bf16[64,192]{1,0:T(8,128)(2,1)S(1)} %finish.1.a0), channel_id=1, source_target_pairs={{0,4},{1,5},{2,6},{3,7},{4,0},{5,1},{6,2},{7,3},{8,12},{9,13},{10,... | collective-permute-start | bytes 73736 | tf_op jit(solution)/shard_map/ppermute | solution.py:427
  144.1 6.4 %collective-permute-start.9 = (f32[64,1536]{1,0:T(8,128)S(1)}, f32[64,1536]{1,0:T(8,128)S(1)}, u32[]{:S(2)}, u32[]{:S(2)}) collective-permute-start(f32[64,1536]{1,0:T(8,128)S(1)} %near.1.own), channel_id=1, source_target_pairs={{0,1},{1,0},{2,3},{3,2},{4,5},{5,4},{6,7},{7,6},{8,9},{9,8},{10,11... | collective-permute-start | bytes 1179656 | tf_op jit(solution)/shard_map/ppermute | solution.py:431
  152.2 18.5 %all-to-all-start.1 = ((bf16[8,64,384]{2,1,0:T(8,128)(2,1)}), bf16[8,64,384]{2,1,0:T(8,128)(2,1)S(1)}, u32[]{:S(2)}, u32[]{:S(2)}) async-start(bf16[8,64,384]{2,1,0:T(8,128)(2,1)} %get-tuple-element.36), calls=%async_computation.1 | async-start | bytes 786432 | tf_op jit(solution)/shard_map/all_to_all | solution.py:491
  155.7 15.1 %collective-permute-start.10 = (bf16[64,192]{1,0:T(8,128)(2,1)S(1)}, bf16[64,192]{1,0:T(8,128)(2,1)S(1)}, u32[]{:S(2)}, u32[]{:S(2)}) collective-permute-start(bf16[64,192]{1,0:T(8,128)(2,1)S(1)} %get-tuple-element.40.q0), channel_id=1, source_target_pairs={{0,8},{8,16},{16,24},{24,0},{32,40},{40,48},{48,56},{56,32},{64,72... | collective-permute-start | bytes 73736 | tf_op jit(solution)/shard_map/ppermute | solution.py:421
  155.7 15.0 %collective-permute-start.11 = (bf16[64,192]{1,0:T(8,128)(2,1)S(1)}, bf16[64,192]{1,0:T(8,128)(2,1)S(1)}, u32[]{:S(2)}, u32[]{:S(2)}) collective-permute-start(bf16[64,192]{1,0:T(8,128)(2,1)S(1)} %get-tuple-element.40.q0), channel_id=1, source_target_pairs={{0,24},{8,0},{16,8},{24,16},{32,56},{40,32},{48,40},{56,48},{64,88... | collective-permute-start | bytes 73736 | tf_op jit(solution)/shard_map/ppermute | solution.py:421
  158.4 12.3 %collective-permute-start.12 = (bf16[64,192]{1,0:T(8,128)(2,1)S(1)}, bf16[64,192]{1,0:T(8,128)(2,1)S(1)}, u32[]{:S(2)}, u32[]{:S(2)}) collective-permute-start(bf16[64,192]{1,0:T(8,128)(2,1)S(1)} %get-tuple-element.40.q0), channel_id=1, source_target_pairs={{0,16},{8,24},{16,0},{24,8},{32,48},{40,56},{48,32},{56,40},{64,80... | collective-permute-start | bytes 73736 | tf_op jit(solution)/shard_map/ppermute | solution.py:421
  170.7 7.3 %copy-start.4 = (bf16[192,1536]{1,0:T(8,128)(2,1)S(1)}, bf16[192,1536]{1,0:T(8,128)(2,1)}, u32[]{:S(2)}) copy-start(bf16[192,1536]{1,0:T(8,128)(2,1)} %w.1) | copy-start | bytes 1769476
  172.3 2.8 %collective-permute-start.13 = (bf16[1,112,128]{2,1,0:T(8,128)(2,1)S(1)}, bf16[1,112,128]{2,1,0:T(8,128)(2,1)S(1)}, u32[]{:S(2)}, u32[]{:S(2)}) collective-permute-start(bf16[1,112,128]{2,1,0:T(8,128)(2,1)S(1)} %get-tuple-element.43), channel_id=1, source_target_pairs={{0,24},{8,0},{16,8},{24,16},{32,56},{40,32},{48,40},{56,48},{64,88... | collective-permute-start | bytes 86024 | tf_op jit(solution)/shard_map/ppermute | solution.py:421
  172.4 3.9 %collective-permute-start.14 = (bf16[1,112,128]{2,1,0:T(8,128)(2,1)S(1)}, bf16[1,112,128]{2,1,0:T(8,128)(2,1)S(1)}, u32[]{:S(2)}, u32[]{:S(2)}) collective-permute-start(bf16[1,112,128]{2,1,0:T(8,128)(2,1)S(1)} %get-tuple-element.42), channel_id=1, source_target_pairs={{0,8},{8,16},{16,24},{24,0},{32,40},{40,48},{48,56},{56,32},{64,72... | collective-permute-start | bytes 86024 | tf_op jit(solution)/shard_map/ppermute | solution.py:421
  173.8 4.2 %collective-permute-start.15 = (bf16[1,112,128]{2,1,0:T(8,128)(2,1)S(1)}, bf16[1,112,128]{2,1,0:T(8,128)(2,1)S(1)}, u32[]{:S(2)}, u32[]{:S(2)}) collective-permute-start(bf16[1,112,128]{2,1,0:T(8,128)(2,1)S(1)} %get-tuple-element.41), channel_id=1, source_target_pairs={{0,16},{8,24},{16,0},{24,8},{32,48},{40,56},{48,32},{56,40},{64,80... | collective-permute-start | bytes 86024 | tf_op jit(solution)/shard_map/ppermute | solution.py:421

commit v3 on v1

--- a/solution.py
+++ b/solution.py
@@ -432,7 +432,7 @@
 
 
 def gather_y(v):
-    return [v] + [permute_y(v, k) for k in SHIFTS]
+    return [v] + [permute_y(v, k) for k in FOREIGN]
 
 
 def body(
@@ -458,7 +458,7 @@
     part_shape = jax.ShapeDtypeStruct((NZ, AUG, 2 * rows), BF16)
     gains = [g.reshape(-1, 128) for g in (gain_in, gain_lat, gain_self)]
 
-    out_near = [cross_out] + [permute_y(cross_out, k) for k in SHIFTS[:2]]
+    out_near = [cross_out] + [permute_y(cross_out, k) for k in FOREIGN[1:]]
     latents_4d = latents.reshape(NZ, NX, rows, depth)
     x = (seq % NX).reshape(1)
     *sent, keys, values_t = encode_call(
@@ -468,7 +468,7 @@
     part = own_call(x, latents_4d, gains[1], cross_query.T, keys, values_t)
     part = plain_call(combine_kernel, "combine", part_shape, part, *parts)
     part, last = lax.optimization_barrier((part, cross_out))
-    out_near.append(permute_y(last, SHIFTS[2]))
+    out_near.insert(1, permute_y(last, FOREIGN[0]))
     lat_rows = lax.dynamic_slice_in_dim(latents, seq * rows, rows, 0)
     part = lax.all_to_all(part, "seq", 0, 0, axis_index_groups=Z_GROUPS)
     part, out_near, lat_rows = lax.optimization_barrier((part, out_near, lat_rows))

time: 190 us -> 191 us (level)
  Pallas kernels: 29.7 us -> 112 us
  starting transfers between devices: 115 us -> 35.9 us
  waiting for transfers between devices: 32.9 us -> 27.2 us
    pallas_call x1, Pallas kernels: 16.8 us -> 78.7 us  [encode_call(): pl.pallas_call(encode_kernel, out_shape=(part, part, part, keys, values_t...]
    ppermute x9, starting transfers between devices: 69.9 us -> 9.78 us  [permute_x(): lax.ppermute(v, 'seq', [(i, i // NX * NX + (i % NX + k) % NX) for i in ra...]
    pallas_call x1, Pallas kernels: 6.83 us -> 27.5 us  [own_call(): pl.pallas_call(own_kernel, out_shape=jax.ShapeDtypeStruct((nz * rows // L...]
    all_to_all x1, starting transfers between devices: 27.9 us -> 8.2 us  [body(): part = lax.all_to_all(part, 'seq', 0, 0, axis_index_groups=Z_GROUPS)]
    ppermute x9, waiting for transfers between devices: 7.11 us -> 4.24 us  [permute_x(): lax.ppermute(v, 'seq', [(i, i // NX * NX + (i % NX + k) % NX) for i in ra...]
    ppermute x6, waiting for transfers between devices: 4.16 us -> 1.31 us  [permute_y(): lax.ppermute(v, 'head', [(i, (i + 2 * k) % (2 * NY)) for i in range(2 * N...]
    all_to_all x1, blocking collectives: 11.1 us -> 13 us  [body(): terms = lax.all_to_all(terms, 'head', 0, 0)]
  transfers between devices with their start and end apart: 18 -> 18, of which waited for: 9 -> 8; matrix products, arithmetic and copies ran while one was open for 1% -> 1% of each run, Pallas kernels for 13% -> 56%
where the time goes in v3:
time: 191 us
  Pallas kernels  112 us (59%)
  starting transfers between devices  35.9 us (19%)
  waiting for transfers between devices  27.2 us (14%)
  blocking collectives  13 us (7%)
  local copies, waits for them, and re-layouts  2.06 us (1%)
    pallas_call x1, Pallas kernels, encode_call(): pl.pallas_call(encode_kernel, out_shape=(part, part, part, keys, values_t...  78.7 us
    pallas_call x1, Pallas kernels, own_call(): pl.pallas_call(own_kernel, out_shape=jax.ShapeDtypeStruct((nz * rows // L...  27.5 us
    all_to_all x1, blocking collectives, body(): terms = lax.all_to_all(terms, 'head', 0, 0)  13 us
    all_to_all x1, waiting for transfers between devices, body(): kv = lax.all_to_all(kv, 'seq', 0, 0, axis_index_groups=Z_GROUPS)  12.2 us
    ppermute x9, starting transfers between devices, permute_x(): lax.ppermute(v, 'seq', [(i, i // NX * NX + (i % NX + k) % NX) for i in ra...  9.78 us
    ppermute x6, starting transfers between devices, permute_y(): lax.ppermute(v, 'head', [(i, (i + 2 * k) % (2 * NY)) for i in range(2 * N...  9.3 us
    all_to_all x1, starting transfers between devices, body(): part = lax.all_to_all(part, 'seq', 0, 0, axis_index_groups=Z_GROUPS)  8.2 us
    all_to_all x1, waiting for transfers between devices, body(): part = lax.all_to_all(part, 'seq', 0, 0, axis_index_groups=Z_GROUPS)  8.07 us
  transfers between devices with their start and end apart: 18, of which 8 were waited for; matrix products, arithmetic and copies ran while one was open for 1% of the time, Pallas kernels for 56%

profile of v3, /device:TPU:1, one launch (start us, length us, event | category | flops | bytes accessed | tf_op | source)
XLA Modules:
  0.0 190.6 jit_solution(6336452900719934820)
XLA Ops:
  0.0 2.1 %collective-permute-start.4 = (bf16[192,1536]{1,0:T(8,128)(2,1)}, bf16[192,1536]{1,0:T(8,128)(2,1)S(1)}, u32[]{:S(2)}, u32[]{:S(2)}) collective-permute-start(bf16[192,1536]{1,0:T(8,128)(2,1)} %w0), channel_id=1, source_target_pairs={{0,2},{1,3},{2,4},{3,5},{4,6},{5,7},{6,0},{7,1},{8,10},{9,11},{10,... | collective-permute-start | bytes 1769480 | tf_op jit(solution)/shard_map/ppermute | solution.py:427
  2.1 1.4 collective-permute-start.5
  3.6 78.7 %encode.1 = (bf16[2,2,112,256]{3,2,1,0:T(8,128)(2,1)}, bf16[2,2,112,256]{3,2,1,0:T(8,128)(2,1)}, bf16[2,2,112,256]{3,2,1,0:T(8,128)(2,1)}, bf16[2048,192]{1,0:T(8,128)(2,1)}, bf16[2,112,2048]{2,1,0:T(8,128)(2,1)}) custom-call(s32[1]{0:T(128)} %bitcast.where, bf16[2048,512]{1,0:T(8,128)(2,1)} %points.1, bf16[8,4,64,1536]{3,2,1,0:T(8,128)(2,1)} %bitcast.17, ...), custom_call_target="tpu_custom_call" | custom-call | flops 16000000000 | bytes 10000000 | tf_op jit(solution)/shard_map/encode/pallas_call | solution.py:264
  82.3 2.8 %collective-permute-start = (bf16[2,2,112,256]{3,2,1,0:T(8,128)(2,1)}, bf16[2,2,112,256]{3,2,1,0:T(8,128)(2,1)S(1)}, u32[]{:S(2)}, u32[]{:S(2)}) collective-permute-start(bf16[2,2,112,256]{3,2,1,0:T(8,128)(2,1)} %get-tuple-element.25), channel_id=1, source_target_pairs={{0,16},{8,24},{16,0},{24,8},{32,48},{40,56},{48,32},{56,40},{64,80... | collective-permute-start | bytes 688136 | tf_op jit(solution)/shard_map/ppermute | solution.py:421
  85.1 0.0 collective-permute-start.1
  85.1 2.7 %collective-permute-start.2 = (bf16[2,2,112,256]{3,2,1,0:T(8,128)(2,1)}, bf16[2,2,112,256]{3,2,1,0:T(8,128)(2,1)S(1)}, u32[]{:S(2)}, u32[]{:S(2)}) collective-permute-start(bf16[2,2,112,256]{3,2,1,0:T(8,128)(2,1)} %get-tuple-element.27), channel_id=1, source_target_pairs={{0,24},{8,0},{16,8},{24,16},{32,56},{40,32},{48,40},{56,48},{64,88... | collective-permute-start | bytes 688136 | tf_op jit(solution)/shard_map/ppermute | solution.py:421
  87.8 27.5 %own.1.a = bf16[2,2,112,256]{3,2,1,0:T(8,128)(2,1)} custom-call(s32[1]{0:T(128)} %bitcast.where, bf16[8,4,64,1536]{3,2,1,0:T(8,128)(2,1)} %bitcast.18, f32[12,128]{1,0:T(8,128)} %bitcast.24, bf16[192,1536]{1,0:T(8,128)(2,1)} %bitcast.20, bf16[2048,192]{1,0:T(8,128)(2,1)} %get-tuple-element.23.keys_in, bf16[2,112,2048]{2,1,0:T(8,128)(2,1)} %get-tuple-element.24.values_in), custom_call_target="tpu_custom_call" | custom-call | flops 4000000000 | bytes 5000000 | tf_op jit(solution)/shard_map/own/pallas_call | solution.py:295
  115.3 0.0 copy-start
  115.3 0.0 collective-permute-done.b
  115.3 0.0 collective-permute-done.1.c
  115.3 0.0 collective-permute-done.2.d
  115.3 0.0 copy-start.6
  115.3 1.0 copy-done.6
  116.3 1.0 combine.1
  117.3 0.0 copy-done
  117.3 1.6 collective-permute-start.3
  119.0 8.2 %all-to-all-start = ((bf16[8,112,128]{2,1,0:T(8,128)(2,1)}), bf16[8,112,128]{2,1,0:T(8,128)(2,1)S(1)}, u32[]{:S(2)}, u32[]{:S(2)}) async-start(bf16[8,112,128]{2,1,0:T(8,128)(2,1)} %combine.1), calls=%async_computation | async-start | bytes 458752 | tf_op jit(solution)/shard_map/all_to_all | solution.py:473
  127.2 0.9 constant_dynamic-slice_fusion.1.latents
  128.1 0.0 collective-permute-done.4.w2
  128.1 0.0 collective-permute-done.5.w3
  128.1 8.1 %all-to-all-done.part = bf16[8,112,128]{2,1,0:T(8,128)(2,1)S(1)} async-done(((bf16[8,112,128]{2,1,0:T(8,128)(2,1)}), bf16[8,112,128]{2,1,0:T(8,128)(2,1)S(1)}, u32[]{:S(2)}, u32[]{:S(2)}) %all-to-all-start) | async-done | bytes 229408 | tf_op jit(solution)/shard_map/all_to_all | solution.py:473
  136.2 0.0 collective-permute-done.3.w1
  136.2 0.2 finish.1.a0
  136.4 0.0 copy-start.1
  136.4 0.0 copy-start.2
  136.5 0.0 copy-start.3
  136.5 0.0 copy-start.5
  136.5 1.4 collective-permute-start.6
  137.9 0.0 collective-permute-start.7
  137.9 2.6 %collective-permute-start.8 = (bf16[64,192]{1,0:T(8,128)(2,1)S(1)}, bf16[64,192]{1,0:T(8,128)(2,1)S(1)}, u32[]{:S(2)}, u32[]{:S(2)}) collective-permute-start(bf16[64,192]{1,0:T(8,128)(2,1)S(1)} %finish.1.a0), channel_id=1, source_target_pairs={{0,6},{1,7},{2,0},{3,1},{4,2},{5,3},{6,4},{7,5},{8,14},{9,15},{10,... | collective-permute-start | bytes 73736 | tf_op jit(solution)/shard_map/ppermute | solution.py:427
  140.6 0.3 collective-permute-done.6.a1
  140.8 1.0 collective-permute-done.7.a2
  141.9 0.0 collective-permute-done.8.a3
  141.9 0.5 near.1.own
  142.4 5.2 %collective-permute-start.9 = (f32[64,1536]{1,0:T(8,128)S(1)}, f32[64,1536]{1,0:T(8,128)S(1)}, u32[]{:S(2)}, u32[]{:S(2)}) collective-permute-start(f32[64,1536]{1,0:T(8,128)S(1)} %near.1.own), channel_id=1, source_target_pairs={{0,1},{1,0},{2,3},{3,2},{4,5},{5,4},{6,7},{7,6},{8,9},{9,8},{10,11... | collective-permute-start | bytes 1179656 | tf_op jit(solution)/shard_map/ppermute | solution.py:431
  147.6 1.3 collective-permute-done.9.other
  148.9 0.0 copy-done.1
  148.9 0.0 copy-done.2
  148.9 0.0 copy-done.3
  148.9 0.0 copy-done.5
  149.0 1.7 middle.1
  150.6 3.5 %all-to-all-start.1 = ((bf16[8,64,384]{2,1,0:T(8,128)(2,1)}), bf16[8,64,384]{2,1,0:T(8,128)(2,1)S(1)}, u32[]{:S(2)}, u32[]{:S(2)}) async-start(bf16[8,64,384]{2,1,0:T(8,128)(2,1)} %get-tuple-element.36), calls=%async_computation.1 | async-start | bytes 786432 | tf_op jit(solution)/shard_map/all_to_all | solution.py:490
  154.1 0.1 collective-permute-start.10
  154.2 2.7 %collective-permute-start.11 = (bf16[64,192]{1,0:T(8,128)(2,1)S(1)}, bf16[64,192]{1,0:T(8,128)(2,1)S(1)}, u32[]{:S(2)}, u32[]{:S(2)}) collective-permute-start(bf16[64,192]{1,0:T(8,128)(2,1)S(1)} %get-tuple-element.40.q0), channel_id=1, source_target_pairs={{0,24},{8,0},{16,8},{24,16},{32,56},{40,32},{48,40},{56,48},{64,88... | collective-permute-start | bytes 73736 | tf_op jit(solution)/shard_map/ppermute | solution.py:421
  156.9 0.0 collective-permute-start.12
  156.9 0.1 constant_dynamic-slice_fusion.mid
  157.0 12.2 %all-to-all-done.1 = bf16[8,64,384]{2,1,0:T(8,128)(2,1)S(1)} async-done(((bf16[8,64,384]{2,1,0:T(8,128)(2,1)}), bf16[8,64,384]{2,1,0:T(8,128)(2,1)S(1)}, u32[]{:S(2)}, u32[]{:S(2)}) %all-to-all-start.1) | async-done | bytes 393248 | tf_op jit(solution)/shard_map/all_to_all | solution.py:490
  169.2 0.0 collective-permute-done.10.q1
  169.2 0.0 collective-permute-done.11.q2
  169.2 0.0 collective-permute-done.12.q3
  169.2 0.0 copy-start.4
  169.2 1.5 self_part.1
  170.7 0.1 collective-permute-start.13
  170.8 1.5 collective-permute-start.14
  172.3 0.0 collective-permute-start.15
  172.3 1.3 collective-permute-done.13.p1
  173.5 1.3 collective-permute-done.14.p2
  174.8 1.7 collective-permute-done.15.p3
  176.5 0.0 copy-done.4
  176.5 0.5 output.1
  177.0 13.0 %all_to_all.15.terms = bf16[8,64,192]{2,1,0:T(8,128)(2,1)S(1)} all-to-all(bf16[8,64,192]{2,1,0:T(8,128)(2,1)S(1)} %output.1), channel_id=1, replica_groups=mesh['seq'=32,'head'=8] {'head'}, dimensions={0} | all-to-all | bytes 393216 | tf_op jit(solution)/shard_map/all_to_all | solution.py:502
  190.0 0.7 add.14
  (1 shorter events, 0.0 us)
Async XLA Ops:
  0.0 128.1 %collective-permute-start.4 = (bf16[192,1536]{1,0:T(8,128)(2,1)}, bf16[192,1536]{1,0:T(8,128)(2,1)S(1)}, u32[]{:S(2)}, u32[]{:S(2)}) collective-permute-start(bf16[192,1536]{1,0:T(8,128)(2,1)} %w0), channel_id=1, source_target_pairs={{0,2},{1,3},{2,4},{3,5},{4,6},{5,7},{6,0},{7,1},{8,10},{9,11},{10,... | collective-permute-start | bytes 1769480 | tf_op jit(solution)/shard_map/ppermute | solution.py:427
  2.1 126.0 %collective-permute-start.5 = (bf16[192,1536]{1,0:T(8,128)(2,1)}, bf16[192,1536]{1,0:T(8,128)(2,1)S(1)}, u32[]{:S(2)}, u32[]{:S(2)}) collective-permute-start(bf16[192,1536]{1,0:T(8,128)(2,1)} %w0), channel_id=1, source_target_pairs={{0,6},{1,7},{2,0},{3,1},{4,2},{5,3},{6,4},{7,5},{8,14},{9,15},{10,... | collective-permute-start | bytes 1769480 | tf_op jit(solution)/shard_map/ppermute | solution.py:427
  82.3 33.0 %collective-permute-start = (bf16[2,2,112,256]{3,2,1,0:T(8,128)(2,1)}, bf16[2,2,112,256]{3,2,1,0:T(8,128)(2,1)S(1)}, u32[]{:S(2)}, u32[]{:S(2)}) collective-permute-start(bf16[2,2,112,256]{3,2,1,0:T(8,128)(2,1)} %get-tuple-element.25), channel_id=1, source_target_pairs={{0,16},{8,24},{16,0},{24,8},{32,48},{40,56},{48,32},{56,40},{64,80... | collective-permute-start | bytes 688136 | tf_op jit(solution)/shard_map/ppermute | solution.py:421
  85.1 30.2 %collective-permute-start.1 = (bf16[2,2,112,256]{3,2,1,0:T(8,128)(2,1)}, bf16[2,2,112,256]{3,2,1,0:T(8,128)(2,1)S(1)}, u32[]{:S(2)}, u32[]{:S(2)}) collective-permute-start(bf16[2,2,112,256]{3,2,1,0:T(8,128)(2,1)} %get-tuple-element.26), channel_id=1, source_target_pairs={{0,8},{8,16},{16,24},{24,0},{32,40},{40,48},{48,56},{56,32},{64,72... | collective-permute-start | bytes 688136 | tf_op jit(solution)/shard_map/ppermute | solution.py:421
  85.1 30.2 %collective-permute-start.2 = (bf16[2,2,112,256]{3,2,1,0:T(8,128)(2,1)}, bf16[2,2,112,256]{3,2,1,0:T(8,128)(2,1)S(1)}, u32[]{:S(2)}, u32[]{:S(2)}) collective-permute-start(bf16[2,2,112,256]{3,2,1,0:T(8,128)(2,1)} %get-tuple-element.27), channel_id=1, source_target_pairs={{0,24},{8,0},{16,8},{24,16},{32,56},{40,32},{48,40},{56,48},{64,88... | collective-permute-start | bytes 688136 | tf_op jit(solution)/shard_map/ppermute | solution.py:421
  115.3 2.1 %copy-start = (bf16[192,1536]{1,0:T(8,128)(2,1)S(1)}, bf16[192,1536]{1,0:T(8,128)(2,1)}, u32[]{:S(2)}) copy-start(bf16[192,1536]{1,0:T(8,128)(2,1)} %w0) | copy-start | bytes 1769476
  115.3 1.0 copy-start.6
  117.3 18.9 %collective-permute-start.3 = (bf16[192,1536]{1,0:T(8,128)(2,1)S(1)}, bf16[192,1536]{1,0:T(8,128)(2,1)S(1)}, u32[]{:S(2)}, u32[]{:S(2)}) collective-permute-start(bf16[192,1536]{1,0:T(8,128)(2,1)S(1)} %copy-done), channel_id=1, source_target_pairs={{0,4},{1,5},{2,6},{3,7},{4,0},{5,1},{6,2},{7,3},{8,12},{9,13},{10,... | collective-permute-start | bytes 1769480 | tf_op jit(solution)/shard_map/ppermute | solution.py:427
  119.0 17.2 %all-to-all-start = ((bf16[8,112,128]{2,1,0:T(8,128)(2,1)}), bf16[8,112,128]{2,1,0:T(8,128)(2,1)S(1)}, u32[]{:S(2)}, u32[]{:S(2)}) async-start(bf16[8,112,128]{2,1,0:T(8,128)(2,1)} %combine.1), calls=%async_computation | async-start | bytes 458752 | tf_op jit(solution)/shard_map/all_to_all | solution.py:473
  136.4 12.5 %copy-start.1 = (bf16[1536,192]{0,1:T(8,128)(2,1)S(1)}, bf16[1536,192]{0,1:T(8,128)(2,1)}, u32[]{:S(2)}) copy-start(bf16[1536,192]{0,1:T(8,128)(2,1)} %param.22) | copy-start | bytes 1769476
  136.4 12.5 %copy-start.2 = (bf16[1536,192]{0,1:T(8,128)(2,1)S(1)}, bf16[1536,192]{0,1:T(8,128)(2,1)}, u32[]{:S(2)}) copy-start(bf16[1536,192]{0,1:T(8,128)(2,1)} %param.23) | copy-start | bytes 1769476
  136.5 12.5 %copy-start.3 = (bf16[1536,192]{0,1:T(8,128)(2,1)S(1)}, bf16[1536,192]{0,1:T(8,128)(2,1)}, u32[]{:S(2)}) copy-start(bf16[1536,192]{0,1:T(8,128)(2,1)} %param.24) | copy-start | bytes 1769476
  136.5 12.5 %copy-start.5 = (f32[1536]{0:T(1024)S(1)}, f32[1536]{0:T(1024)}, u32[]{:S(2)}) copy-start(f32[1536]{0:T(1024)} %param.17) | copy-start | bytes 18436
  136.5 4.4 %collective-permute-start.6 = (bf16[64,192]{1,0:T(8,128)(2,1)S(1)}, bf16[64,192]{1,0:T(8,128)(2,1)S(1)}, u32[]{:S(2)}, u32[]{:S(2)}) collective-permute-start(bf16[64,192]{1,0:T(8,128)(2,1)S(1)} %finish.1.a0), channel_id=1, source_target_pairs={{0,4},{1,5},{2,6},{3,7},{4,0},{5,1},{6,2},{7,3},{8,12},{9,13},{10,... | collective-permute-start | bytes 73736 | tf_op jit(solution)/shard_map/ppermute | solution.py:427
  137.9 4.0 %collective-permute-start.7 = (bf16[64,192]{1,0:T(8,128)(2,1)S(1)}, bf16[64,192]{1,0:T(8,128)(2,1)S(1)}, u32[]{:S(2)}, u32[]{:S(2)}) collective-permute-start(bf16[64,192]{1,0:T(8,128)(2,1)S(1)} %finish.1.a0), channel_id=1, source_target_pairs={{0,2},{1,3},{2,4},{3,5},{4,6},{5,7},{6,0},{7,1},{8,10},{9,11},{10,... | collective-permute-start | bytes 73736 | tf_op jit(solution)/shard_map/ppermute | solution.py:427
  137.9 3.9 %collective-permute-start.8 = (bf16[64,192]{1,0:T(8,128)(2,1)S(1)}, bf16[64,192]{1,0:T(8,128)(2,1)S(1)}, u32[]{:S(2)}, u32[]{:S(2)}) collective-permute-start(bf16[64,192]{1,0:T(8,128)(2,1)S(1)} %finish.1.a0), channel_id=1, source_target_pairs={{0,6},{1,7},{2,0},{3,1},{4,2},{5,3},{6,4},{7,5},{8,14},{9,15},{10,... | collective-permute-start | bytes 73736 | tf_op jit(solution)/shard_map/ppermute | solution.py:427
  142.4 6.5 %collective-permute-start.9 = (f32[64,1536]{1,0:T(8,128)S(1)}, f32[64,1536]{1,0:T(8,128)S(1)}, u32[]{:S(2)}, u32[]{:S(2)}) collective-permute-start(f32[64,1536]{1,0:T(8,128)S(1)} %near.1.own), channel_id=1, source_target_pairs={{0,1},{1,0},{2,3},{3,2},{4,5},{5,4},{6,7},{7,6},{8,9},{9,8},{10,11... | collective-permute-start | bytes 1179656 | tf_op jit(solution)/shard_map/ppermute | solution.py:431
  150.6 18.5 %all-to-all-start.1 = ((bf16[8,64,384]{2,1,0:T(8,128)(2,1)}), bf16[8,64,384]{2,1,0:T(8,128)(2,1)S(1)}, u32[]{:S(2)}, u32[]{:S(2)}) async-start(bf16[8,64,384]{2,1,0:T(8,128)(2,1)} %get-tuple-element.36), calls=%async_computation.1 | async-start | bytes 786432 | tf_op jit(solution)/shard_map/all_to_all | solution.py:490
  154.1 15.1 %collective-permute-start.10 = (bf16[64,192]{1,0:T(8,128)(2,1)S(1)}, bf16[64,192]{1,0:T(8,128)(2,1)S(1)}, u32[]{:S(2)}, u32[]{:S(2)}) collective-permute-start(bf16[64,192]{1,0:T(8,128)(2,1)S(1)} %get-tuple-element.40.q0), channel_id=1, source_target_pairs={{0,8},{8,16},{16,24},{24,0},{32,40},{40,48},{48,56},{56,32},{64,72... | collective-permute-start | bytes 73736 | tf_op jit(solution)/shard_map/ppermute | solution.py:421
  154.2 15.0 %collective-permute-start.11 = (bf16[64,192]{1,0:T(8,128)(2,1)S(1)}, bf16[64,192]{1,0:T(8,128)(2,1)S(1)}, u32[]{:S(2)}, u32[]{:S(2)}) collective-permute-start(bf16[64,192]{1,0:T(8,128)(2,1)S(1)} %get-tuple-element.40.q0), channel_id=1, source_target_pairs={{0,24},{8,0},{16,8},{24,16},{32,56},{40,32},{48,40},{56,48},{64,88... | collective-permute-start | bytes 73736 | tf_op jit(solution)/shard_map/ppermute | solution.py:421
  156.9 12.3 %collective-permute-start.12 = (bf16[64,192]{1,0:T(8,128)(2,1)S(1)}, bf16[64,192]{1,0:T(8,128)(2,1)S(1)}, u32[]{:S(2)}, u32[]{:S(2)}) collective-permute-start(bf16[64,192]{1,0:T(8,128)(2,1)S(1)} %get-tuple-element.40.q0), channel_id=1, source_target_pairs={{0,16},{8,24},{16,0},{24,8},{32,48},{40,56},{48,32},{56,40},{64,80... | collective-permute-start | bytes 73736 | tf_op jit(solution)/shard_map/ppermute | solution.py:421
  169.2 7.3 %copy-start.4 = (bf16[192,1536]{1,0:T(8,128)(2,1)S(1)}, bf16[192,1536]{1,0:T(8,128)(2,1)}, u32[]{:S(2)}) copy-start(bf16[192,1536]{1,0:T(8,128)(2,1)} %w.1) | copy-start | bytes 1769476
  170.7 2.8 %collective-permute-start.13 = (bf16[1,112,128]{2,1,0:T(8,128)(2,1)S(1)}, bf16[1,112,128]{2,1,0:T(8,128)(2,1)S(1)}, u32[]{:S(2)}, u32[]{:S(2)}) collective-permute-start(bf16[1,112,128]{2,1,0:T(8,128)(2,1)S(1)} %get-tuple-element.43), channel_id=1, source_target_pairs={{0,24},{8,0},{16,8},{24,16},{32,56},{40,32},{48,40},{56,48},{64,88... | collective-permute-start | bytes 86024 | tf_op jit(solution)/shard_map/ppermute | solution.py:421
  170.8 4.0 %collective-permute-start.14 = (bf16[1,112,128]{2,1,0:T(8,128)(2,1)S(1)}, bf16[1,112,128]{2,1,0:T(8,128)(2,1)S(1)}, u32[]{:S(2)}, u32[]{:S(2)}) collective-permute-start(bf16[1,112,128]{2,1,0:T(8,128)(2,1)S(1)} %get-tuple-element.42), channel_id=1, source_target_pairs={{0,8},{8,16},{16,24},{24,0},{32,40},{40,48},{48,56},{56,32},{64,72... | collective-permute-start | bytes 86024 | tf_op jit(solution)/shard_map/ppermute | solution.py:421
  172.3 4.2 %collective-permute-start.15 = (bf16[1,112,128]{2,1,0:T(8,128)(2,1)S(1)}, bf16[1,112,128]{2,1,0:T(8,128)(2,1)S(1)}, u32[]{:S(2)}, u32[]{:S(2)}) collective-permute-start(bf16[1,112,128]{2,1,0:T(8,128)(2,1)S(1)} %get-tuple-element.41), channel_id=1, source_target_pairs={{0,16},{8,24},{16,0},{24,8},{32,48},{40,56},{48,32},{56,40},{64,80... | collective-permute-start | bytes 86024 | tf_op jit(solution)/shard_map/ppermute | solution.py:421

commit v4 on v2

--- a/solution.py
+++ b/solution.py
@@ -155,9 +155,10 @@
         lax.fori_loop(0, blocks, again, 0)
 
 
-def norm_rows(lbuf, row, xbuf):
+def norm_rows(lbuf, row, xbuf, ready=lambda z: None):
     rows, width = lbuf.shape[1], lbuf.shape[2]
     for z in range(lbuf.shape[0]):
+        ready(z)
         part = pl.ds(z * rows, rows)
         x = lbuf[z].astype(F32)
         off = x - x[:, 0:1]
@@ -220,19 +221,21 @@
     where, latents, gain, wq_in, keys_in, values_in, out,
     lbuf, gbuf, wq, keys, values_t, xbuf, qbuf, sbuf, pbuf, sems,
 ):
+    nz = lbuf.shape[0]
     copies = fetch(
-        [(latents.at[:, where[0]], lbuf), (gain, gbuf), (wq_in, wq), (keys_in, keys), (values_in, values_t)],
+        [(gain, gbuf)]
+        + [(latents.at[z, where[0]], lbuf.at[z]) for z in range(nz)]
+        + [(wq_in, wq), (keys_in, keys), (values_in, values_t)],
         sems,
     )
     for copy in copies:
         copy.start()
     copies[0].wait()
-    copies[1].wait()
-    norm_rows(lbuf, gain_row(gbuf), xbuf)
-    copies[2].wait()
+    norm_rows(lbuf, gain_row(gbuf), xbuf, lambda z: copies[1 + z].wait())
+    copies[1 + nz].wait()
     project_query(xbuf, wq, qbuf)
-    copies[3].wait()
-    copies[4].wait()
+    copies[2 + nz].wait()
+    copies[3 + nz].wait()
     attend_chunk(qbuf, keys, values_t, sbuf, pbuf, out)
 
 
@@ -307,7 +310,7 @@
             pltpu.VMEM((nz * rows, 2 * HS), BF16),
         ]
         + attend_scratch(keys.shape[0])
-        + [pltpu.SemaphoreType.DMA((5,))],
+        + [pltpu.SemaphoreType.DMA((nz + 4,))],
         compiler_params=pltpu.CompilerParams(vmem_limit_bytes=VMEM_WIDE),
         cost_estimate=pl.CostEstimate(
             flops=4 * 10**9, bytes_accessed=5 * 10**6, transcendentals=2 * 10**6

time: 191 us -> 190 us (level)
  starting transfers between devices: 34.4 us -> 119 us
  Pallas kernels: 112 us -> 30.1 us
  waiting for transfers between devices: 30.2 us -> 27.4 us
    ppermute x9, starting transfers between devices: 9.79 us -> 77.5 us  [permute_x(): lax.ppermute(v, 'seq', [(i, i // NX * NX + (i % NX + k) % NX) for i in ra...]
    pallas_call x1, Pallas kernels: 78.7 us -> 16.8 us  [encode_call(): pl.pallas_call(encode_kernel, out_shape=(part, part, part, keys, values_t...]
    pallas_call x1, Pallas kernels: 27.5 us -> 7.19 us  [own_call(): pl.pallas_call(own_kernel, out_shape=jax.ShapeDtypeStruct((nz * rows // L...]
    all_to_all x1, starting transfers between devices: 8.2 us -> 24.6 us  [body(): part = lax.all_to_all(part, 'seq', 0, 0, axis_index_groups=Z_GROUPS)]
    all_to_all x1, waiting for transfers between devices: 12.2 us -> 9.95 us  [body(): kv = lax.all_to_all(kv, 'seq', 0, 0, axis_index_groups=Z_GROUPS)]
  transfers between devices with their start and end apart: 18 -> 18, of which waited for: 8 -> 8; matrix products, arithmetic and copies ran while one was open for 1% -> 1% of each run, Pallas kernels for 56% -> 13%
where the time goes in v4:
time: 190 us; the launch traced here: 189 us
  starting transfers between devices  119 us (63%)
  Pallas kernels  30.1 us (16%)
  waiting for transfers between devices  27.4 us (14%)
  blocking collectives  10.8 us (6%)
  local copies, waits for them, and re-layouts  2.01 us (1%)
    ppermute x9, starting transfers between devices, permute_x(): lax.ppermute(v, 'seq', [(i, i // NX * NX + (i % NX + k) % NX) for i in ra...  77.5 us
    all_to_all x1, starting transfers between devices, body(): part = lax.all_to_all(part, 'seq', 0, 0, axis_index_groups=Z_GROUPS)  24.6 us
    pallas_call x1, Pallas kernels, encode_call(): pl.pallas_call(encode_kernel, out_shape=(part, part, part, keys, values_t...  16.8 us
    all_to_all x1, blocking collectives, body(): terms = lax.all_to_all(terms, 'head', 0, 0)  10.8 us
    all_to_all x1, waiting for transfers between devices, body(): kv = lax.all_to_all(kv, 'seq', 0, 0, axis_index_groups=Z_GROUPS)  9.95 us
    all_to_all x1, waiting for transfers between devices, body(): part = lax.all_to_all(part, 'seq', 0, 0, axis_index_groups=Z_GROUPS)  8.08 us
    ppermute x6, starting transfers between devices, permute_y(): lax.ppermute(v, 'head', [(i, (i + 2 * k) % (2 * NY)) for i in range(2 * N...  8.03 us
    pallas_call x1, Pallas kernels, own_call(): pl.pallas_call(own_kernel, out_shape=jax.ShapeDtypeStruct((nz * rows // L...  7.19 us
  transfers between devices with their start and end apart: 18, of which 8 were waited for; matrix products, arithmetic and copies ran while one was open for 1% of the time, Pallas kernels for 13%

profile of v4, /device:TPU:1, one launch (start us, length us, event | category | flops | bytes accessed | tf_op | source)
XLA Modules:
  0.0 189.2 jit_solution(5728053413737428089)
XLA Ops:
  0.0 2.1 %collective-permute-start.3 = (bf16[192,1536]{1,0:T(8,128)(2,1)}, bf16[192,1536]{1,0:T(8,128)(2,1)S(1)}, u32[]{:S(2)}, u32[]{:S(2)}) collective-permute-start(bf16[192,1536]{1,0:T(8,128)(2,1)} %w0), channel_id=1, source_target_pairs={{0,2},{1,3},{2,4},{3,5},{4,6},{5,7},{6,0},{7,1},{8,10},{9,11},{10,... | collective-permute-start | bytes 1769480 | tf_op jit(solution)/shard_map/ppermute | solution.py:430
  2.1 1.4 collective-permute-start.4
  3.6 16.8 %encode.1 = (bf16[2,2,112,256]{3,2,1,0:T(8,128)(2,1)}, bf16[2,2,112,256]{3,2,1,0:T(8,128)(2,1)}, bf16[2,2,112,256]{3,2,1,0:T(8,128)(2,1)}, bf16[2048,192]{1,0:T(8,128)(2,1)}, bf16[2,112,2048]{2,1,0:T(8,128)(2,1)}) custom-call(s32[1]{0:T(128)} %bitcast.where, bf16[2048,512]{1,0:T(8,128)(2,1)} %points.1, bf16[8,4,64,1536]{3,2,1,0:T(8,128)(2,1)} %bitcast.17, ...), custom_call_target="tpu_custom_call" | custom-call | flops 16000000000 | bytes 10000000 | tf_op jit(solution)/shard_map/encode/pallas_call | solution.py:267
  20.4 64.8 %collective-permute-start = (bf16[2,2,112,256]{3,2,1,0:T(8,128)(2,1)}, bf16[2,2,112,256]{3,2,1,0:T(8,128)(2,1)S(1)}, u32[]{:S(2)}, u32[]{:S(2)}) collective-permute-start(bf16[2,2,112,256]{3,2,1,0:T(8,128)(2,1)} %get-tuple-element.25), channel_id=1, source_target_pairs={{0,16},{8,24},{16,0},{24,8},{32,48},{40,56},{48,32},{56,40},{64,80... | collective-permute-start | bytes 688136 | tf_op jit(solution)/shard_map/ppermute | solution.py:424
  85.1 0.3 collective-permute-start.1
  85.4 2.3 %collective-permute-start.2 = (bf16[2,2,112,256]{3,2,1,0:T(8,128)(2,1)}, bf16[2,2,112,256]{3,2,1,0:T(8,128)(2,1)S(1)}, u32[]{:S(2)}, u32[]{:S(2)}) collective-permute-start(bf16[2,2,112,256]{3,2,1,0:T(8,128)(2,1)} %get-tuple-element.27), channel_id=1, source_target_pairs={{0,24},{8,0},{16,8},{24,16},{32,56},{40,32},{48,40},{56,48},{64,88... | collective-permute-start | bytes 688136 | tf_op jit(solution)/shard_map/ppermute | solution.py:424
  87.8 7.2 %own.1.a = bf16[2,2,112,256]{3,2,1,0:T(8,128)(2,1)} custom-call(s32[1]{0:T(128)} %bitcast.where, bf16[8,4,64,1536]{3,2,1,0:T(8,128)(2,1)} %bitcast.18, f32[12,128]{1,0:T(8,128)} %bitcast.24, bf16[192,1536]{1,0:T(8,128)(2,1)} %bitcast.20, bf16[2048,192]{1,0:T(8,128)(2,1)} %get-tuple-element.23.keys_in, bf16[2,112,2048]{2,1,0:T(8,128)(2,1)} %get-tuple-element.24.values_in), custom_call_target="tpu_custom_call" | custom-call | flops 4000000000 | bytes 5000000 | tf_op jit(solution)/shard_map/own/pallas_call | solution.py:298
  95.0 0.0 copy-start
  95.0 0.0 collective-permute-done.b
  95.0 0.8 collective-permute-done.1.c
  95.8 0.0 collective-permute-done.2.d
  95.8 0.0 copy-start.6
  95.8 0.9 copy-done.6
  96.7 1.0 combine.1
  97.8 0.0 copy-done
  97.8 1.6 collective-permute-start.5
  99.3 24.6 %all-to-all-start = ((bf16[8,112,128]{2,1,0:T(8,128)(2,1)}), bf16[8,112,128]{2,1,0:T(8,128)(2,1)S(1)}, u32[]{:S(2)}, u32[]{:S(2)}) async-start(bf16[8,112,128]{2,1,0:T(8,128)(2,1)} %combine.1), calls=%async_computation | async-start | bytes 458752 | tf_op jit(solution)/shard_map/all_to_all | solution.py:477
  124.0 0.9 constant_dynamic-slice_fusion.1.latents
  124.9 0.0 collective-permute-done.3.w1
  124.9 0.0 collective-permute-done.4.w2
  124.9 8.1 %all-to-all-done.part = bf16[8,112,128]{2,1,0:T(8,128)(2,1)S(1)} async-done(((bf16[8,112,128]{2,1,0:T(8,128)(2,1)}), bf16[8,112,128]{2,1,0:T(8,128)(2,1)S(1)}, u32[]{:S(2)}, u32[]{:S(2)}) %all-to-all-start) | async-done | bytes 229408 | tf_op jit(solution)/shard_map/all_to_all | solution.py:477
  133.0 0.0 collective-permute-done.5.w3
  133.0 0.2 finish.1.a0
  133.2 0.0 copy-start.1
  133.3 0.0 copy-start.2
  133.3 0.0 copy-start.3
  133.3 0.0 copy-start.5
  133.3 0.5 collective-permute-start.6
  133.8 2.3 %collective-permute-start.7 = (bf16[64,192]{1,0:T(8,128)(2,1)S(1)}, bf16[64,192]{1,0:T(8,128)(2,1)S(1)}, u32[]{:S(2)}, u32[]{:S(2)}) collective-permute-start(bf16[64,192]{1,0:T(8,128)(2,1)S(1)} %finish.1.a0), channel_id=1, source_target_pairs={{0,6},{1,7},{2,0},{3,1},{4,2},{5,3},{6,4},{7,5},{8,14},{9,15},{10,... | collective-permute-start | bytes 73736 | tf_op jit(solution)/shard_map/ppermute | solution.py:430
  136.0 0.1 collective-permute-start.8
  136.2 1.2 collective-permute-done.6.a1
  137.3 0.0 collective-permute-done.7.a2
  137.3 3.1 %collective-permute-done.8.a3 = bf16[64,192]{1,0:T(8,128)(2,1)S(1)} collective-permute-done((bf16[64,192]{1,0:T(8,128)(2,1)S(1)}, bf16[64,192]{1,0:T(8,128)(2,1)S(1)}, u32[]{:S(2)}, u32[]{:S(2)}) %collective-permute-start.8) | collective-permute-done | bytes 24608 | tf_op jit(solution)/shard_map/ppermute | solution.py:430
  140.4 0.5 near.1.own
  141.0 5.1 %collective-permute-start.9 = (f32[64,1536]{1,0:T(8,128)S(1)}, f32[64,1536]{1,0:T(8,128)S(1)}, u32[]{:S(2)}, u32[]{:S(2)}) collective-permute-start(f32[64,1536]{1,0:T(8,128)S(1)} %near.1.own), channel_id=1, source_target_pairs={{0,1},{1,0},{2,3},{3,2},{4,5},{5,4},{6,7},{7,6},{8,9},{9,8},{10,11... | collective-permute-start | bytes 1179656 | tf_op jit(solution)/shard_map/ppermute | solution.py:434
  146.1 1.3 collective-permute-done.9.other
  147.5 0.0 copy-done.1
  147.5 0.0 copy-done.2
  147.5 0.0 copy-done.3
  147.5 0.0 copy-done.5
  147.5 1.7 middle.1
  149.2 3.5 %all-to-all-start.1 = ((bf16[8,64,384]{2,1,0:T(8,128)(2,1)}), bf16[8,64,384]{2,1,0:T(8,128)(2,1)S(1)}, u32[]{:S(2)}, u32[]{:S(2)}) async-start(bf16[8,64,384]{2,1,0:T(8,128)(2,1)} %get-tuple-element.36), calls=%async_computation.1 | async-start | bytes 786432 | tf_op jit(solution)/shard_map/all_to_all | solution.py:494
  152.6 3.2 %collective-permute-start.10 = (bf16[64,192]{1,0:T(8,128)(2,1)S(1)}, bf16[64,192]{1,0:T(8,128)(2,1)S(1)}, u32[]{:S(2)}, u32[]{:S(2)}) collective-permute-start(bf16[64,192]{1,0:T(8,128)(2,1)S(1)} %get-tuple-element.40.q0), channel_id=1, source_target_pairs={{0,8},{8,16},{16,24},{24,0},{32,40},{40,48},{48,56},{56,32},{64,72... | collective-permute-start | bytes 73736 | tf_op jit(solution)/shard_map/ppermute | solution.py:424
  155.8 0.7 collective-permute-start.11
  156.5 1.2 collective-permute-start.12
  157.7 0.1 constant_dynamic-slice_fusion.mid
  157.7 10.0 %all-to-all-done.1 = bf16[8,64,384]{2,1,0:T(8,128)(2,1)S(1)} async-done(((bf16[8,64,384]{2,1,0:T(8,128)(2,1)}), bf16[8,64,384]{2,1,0:T(8,128)(2,1)S(1)}, u32[]{:S(2)}, u32[]{:S(2)}) %all-to-all-start.1) | async-done | bytes 393248 | tf_op jit(solution)/shard_map/all_to_all | solution.py:494
  167.7 0.0 collective-permute-done.10.q1
  167.7 0.0 collective-permute-done.11.q2
  167.7 0.0 collective-permute-done.12.q3
  167.7 0.0 copy-start.4
  167.7 1.5 self_part.1
  169.2 3.8 %collective-permute-start.13 = (bf16[1,112,128]{2,1,0:T(8,128)(2,1)S(1)}, bf16[1,112,128]{2,1,0:T(8,128)(2,1)S(1)}, u32[]{:S(2)}, u32[]{:S(2)}) collective-permute-start(bf16[1,112,128]{2,1,0:T(8,128)(2,1)S(1)} %get-tuple-element.43), channel_id=1, source_target_pairs={{0,24},{8,0},{16,8},{24,16},{32,56},{40,32},{48,40},{56,48},{64,88... | collective-permute-start | bytes 86024 | tf_op jit(solution)/shard_map/ppermute | solution.py:424
  173.0 0.0 collective-permute-start.14
  173.0 1.3 collective-permute-start.15
  174.3 0.0 collective-permute-done.13.p1
  174.3 2.7 %collective-permute-done.14.p2 = bf16[1,112,128]{2,1,0:T(8,128)(2,1)S(1)} collective-permute-done((bf16[1,112,128]{2,1,0:T(8,128)(2,1)S(1)}, bf16[1,112,128]{2,1,0:T(8,128)(2,1)S(1)}, u32[]{:S(2)}, u32[]{:S(2)}) %collective-permute-start.14) | collective-permute-done | bytes 28704 | tf_op jit(solution)/shard_map/ppermute | solution.py:424
  177.0 0.3 collective-permute-done.15.p3
  177.3 0.0 copy-done.4
  177.3 0.5 output.1
  177.7 10.8 %all_to_all.15.terms = bf16[8,64,192]{2,1,0:T(8,128)(2,1)S(1)} all-to-all(bf16[8,64,192]{2,1,0:T(8,128)(2,1)S(1)} %output.1), channel_id=1, replica_groups=mesh['seq'=32,'head'=8] {'head'}, dimensions={0} | all-to-all | bytes 393216 | tf_op jit(solution)/shard_map/all_to_all | solution.py:506
  188.5 0.7 add.14
  (1 shorter events, 0.0 us)
Async XLA Ops:
  0.0 124.9 %collective-permute-start.3 = (bf16[192,1536]{1,0:T(8,128)(2,1)}, bf16[192,1536]{1,0:T(8,128)(2,1)S(1)}, u32[]{:S(2)}, u32[]{:S(2)}) collective-permute-start(bf16[192,1536]{1,0:T(8,128)(2,1)} %w0), channel_id=1, source_target_pairs={{0,2},{1,3},{2,4},{3,5},{4,6},{5,7},{6,0},{7,1},{8,10},{9,11},{10,... | collective-permute-start | bytes 1769480 | tf_op jit(solution)/shard_map/ppermute | solution.py:430
  2.1 122.8 %collective-permute-start.4 = (bf16[192,1536]{1,0:T(8,128)(2,1)}, bf16[192,1536]{1,0:T(8,128)(2,1)S(1)}, u32[]{:S(2)}, u32[]{:S(2)}) collective-permute-start(bf16[192,1536]{1,0:T(8,128)(2,1)} %w0), channel_id=1, source_target_pairs={{0,6},{1,7},{2,0},{3,1},{4,2},{5,3},{6,4},{7,5},{8,14},{9,15},{10,... | collective-permute-start | bytes 1769480 | tf_op jit(solution)/shard_map/ppermute | solution.py:430
  20.4 74.6 %collective-permute-start = (bf16[2,2,112,256]{3,2,1,0:T(8,128)(2,1)}, bf16[2,2,112,256]{3,2,1,0:T(8,128)(2,1)S(1)}, u32[]{:S(2)}, u32[]{:S(2)}) collective-permute-start(bf16[2,2,112,256]{3,2,1,0:T(8,128)(2,1)} %get-tuple-element.25), channel_id=1, source_target_pairs={{0,16},{8,24},{16,0},{24,8},{32,48},{40,56},{48,32},{56,40},{64,80... | collective-permute-start | bytes 688136 | tf_op jit(solution)/shard_map/ppermute | solution.py:424
  85.1 10.7 %collective-permute-start.1 = (bf16[2,2,112,256]{3,2,1,0:T(8,128)(2,1)}, bf16[2,2,112,256]{3,2,1,0:T(8,128)(2,1)S(1)}, u32[]{:S(2)}, u32[]{:S(2)}) collective-permute-start(bf16[2,2,112,256]{3,2,1,0:T(8,128)(2,1)} %get-tuple-element.26), channel_id=1, source_target_pairs={{0,8},{8,16},{16,24},{24,0},{32,40},{40,48},{48,56},{56,32},{64,72... | collective-permute-start | bytes 688136 | tf_op jit(solution)/shard_map/ppermute | solution.py:424
  85.4 10.3 %collective-permute-start.2 = (bf16[2,2,112,256]{3,2,1,0:T(8,128)(2,1)}, bf16[2,2,112,256]{3,2,1,0:T(8,128)(2,1)S(1)}, u32[]{:S(2)}, u32[]{:S(2)}) collective-permute-start(bf16[2,2,112,256]{3,2,1,0:T(8,128)(2,1)} %get-tuple-element.27), channel_id=1, source_target_pairs={{0,24},{8,0},{16,8},{24,16},{32,56},{40,32},{48,40},{56,48},{64,88... | collective-permute-start | bytes 688136 | tf_op jit(solution)/shard_map/ppermute | solution.py:424
  95.0 2.8 %copy-start = (bf16[192,1536]{1,0:T(8,128)(2,1)S(1)}, bf16[192,1536]{1,0:T(8,128)(2,1)}, u32[]{:S(2)}) copy-start(bf16[192,1536]{1,0:T(8,128)(2,1)} %w0) | copy-start | bytes 1769476
  95.8 0.9 copy-start.6
  97.8 35.3 %collective-permute-start.5 = (bf16[192,1536]{1,0:T(8,128)(2,1)S(1)}, bf16[192,1536]{1,0:T(8,128)(2,1)S(1)}, u32[]{:S(2)}, u32[]{:S(2)}) collective-permute-start(bf16[192,1536]{1,0:T(8,128)(2,1)S(1)} %copy-done), channel_id=1, source_target_pairs={{0,4},{1,5},{2,6},{3,7},{4,0},{5,1},{6,2},{7,3},{8,12},{9,13},{10,... | collective-permute-start | bytes 1769480 | tf_op jit(solution)/shard_map/ppermute | solution.py:430
  99.3 33.7 %all-to-all-start = ((bf16[8,112,128]{2,1,0:T(8,128)(2,1)}), bf16[8,112,128]{2,1,0:T(8,128)(2,1)S(1)}, u32[]{:S(2)}, u32[]{:S(2)}) async-start(bf16[8,112,128]{2,1,0:T(8,128)(2,1)} %combine.1), calls=%async_computation | async-start | bytes 458752 | tf_op jit(solution)/shard_map/all_to_all | solution.py:477
  133.2 14.2 %copy-start.1 = (bf16[1536,192]{0,1:T(8,128)(2,1)S(1)}, bf16[1536,192]{0,1:T(8,128)(2,1)}, u32[]{:S(2)}) copy-start(bf16[1536,192]{0,1:T(8,128)(2,1)} %param.22) | copy-start | bytes 1769476
  133.3 14.2 %copy-start.2 = (bf16[1536,192]{0,1:T(8,128)(2,1)S(1)}, bf16[1536,192]{0,1:T(8,128)(2,1)}, u32[]{:S(2)}) copy-start(bf16[1536,192]{0,1:T(8,128)(2,1)} %param.23) | copy-start | bytes 1769476
  133.3 14.2 %copy-start.3 = (bf16[1536,192]{0,1:T(8,128)(2,1)S(1)}, bf16[1536,192]{0,1:T(8,128)(2,1)}, u32[]{:S(2)}) copy-start(bf16[1536,192]{0,1:T(8,128)(2,1)} %param.24) | copy-start | bytes 1769476
  133.3 14.2 %copy-start.5 = (f32[1536]{0:T(1024)S(1)}, f32[1536]{0:T(1024)}, u32[]{:S(2)}) copy-start(f32[1536]{0:T(1024)} %param.17) | copy-start | bytes 18436
  133.3 4.1 %collective-permute-start.6 = (bf16[64,192]{1,0:T(8,128)(2,1)S(1)}, bf16[64,192]{1,0:T(8,128)(2,1)S(1)}, u32[]{:S(2)}, u32[]{:S(2)}) collective-permute-start(bf16[64,192]{1,0:T(8,128)(2,1)S(1)} %finish.1.a0), channel_id=1, source_target_pairs={{0,2},{1,3},{2,4},{3,5},{4,6},{5,7},{6,0},{7,1},{8,10},{9,11},{10,... | collective-permute-start | bytes 73736 | tf_op jit(solution)/shard_map/ppermute | solution.py:430
  133.8 3.6 %collective-permute-start.7 = (bf16[64,192]{1,0:T(8,128)(2,1)S(1)}, bf16[64,192]{1,0:T(8,128)(2,1)S(1)}, u32[]{:S(2)}, u32[]{:S(2)}) collective-permute-start(bf16[64,192]{1,0:T(8,128)(2,1)S(1)} %finish.1.a0), channel_id=1, source_target_pairs={{0,6},{1,7},{2,0},{3,1},{4,2},{5,3},{6,4},{7,5},{8,14},{9,15},{10,... | collective-permute-start | bytes 73736 | tf_op jit(solution)/shard_map/ppermute | solution.py:430
  136.0 4.4 %collective-permute-start.8 = (bf16[64,192]{1,0:T(8,128)(2,1)S(1)}, bf16[64,192]{1,0:T(8,128)(2,1)S(1)}, u32[]{:S(2)}, u32[]{:S(2)}) collective-permute-start(bf16[64,192]{1,0:T(8,128)(2,1)S(1)} %finish.1.a0), channel_id=1, source_target_pairs={{0,4},{1,5},{2,6},{3,7},{4,0},{5,1},{6,2},{7,3},{8,12},{9,13},{10,... | collective-permute-start | bytes 73736 | tf_op jit(solution)/shard_map/ppermute | solution.py:430
  141.0 6.5 %collective-permute-start.9 = (f32[64,1536]{1,0:T(8,128)S(1)}, f32[64,1536]{1,0:T(8,128)S(1)}, u32[]{:S(2)}, u32[]{:S(2)}) collective-permute-start(f32[64,1536]{1,0:T(8,128)S(1)} %near.1.own), channel_id=1, source_target_pairs={{0,1},{1,0},{2,3},{3,2},{4,5},{5,4},{6,7},{7,6},{8,9},{9,8},{10,11... | collective-permute-start | bytes 1179656 | tf_op jit(solution)/shard_map/ppermute | solution.py:434
  149.2 18.5 %all-to-all-start.1 = ((bf16[8,64,384]{2,1,0:T(8,128)(2,1)}), bf16[8,64,384]{2,1,0:T(8,128)(2,1)S(1)}, u32[]{:S(2)}, u32[]{:S(2)}) async-start(bf16[8,64,384]{2,1,0:T(8,128)(2,1)} %get-tuple-element.36), calls=%async_computation.1 | async-start | bytes 786432 | tf_op jit(solution)/shard_map/all_to_all | solution.py:494
  152.6 15.1 %collective-permute-start.10 = (bf16[64,192]{1,0:T(8,128)(2,1)S(1)}, bf16[64,192]{1,0:T(8,128)(2,1)S(1)}, u32[]{:S(2)}, u32[]{:S(2)}) collective-permute-start(bf16[64,192]{1,0:T(8,128)(2,1)S(1)} %get-tuple-element.40.q0), channel_id=1, source_target_pairs={{0,8},{8,16},{16,24},{24,0},{32,40},{40,48},{48,56},{56,32},{64,72... | collective-permute-start | bytes 73736 | tf_op jit(solution)/shard_map/ppermute | solution.py:424
  155.8 11.9 %collective-permute-start.11 = (bf16[64,192]{1,0:T(8,128)(2,1)S(1)}, bf16[64,192]{1,0:T(8,128)(2,1)S(1)}, u32[]{:S(2)}, u32[]{:S(2)}) collective-permute-start(bf16[64,192]{1,0:T(8,128)(2,1)S(1)} %get-tuple-element.40.q0), channel_id=1, source_target_pairs={{0,24},{8,0},{16,8},{24,16},{32,56},{40,32},{48,40},{56,48},{64,88... | collective-permute-start | bytes 73736 | tf_op jit(solution)/shard_map/ppermute | solution.py:424
  156.5 11.2 %collective-permute-start.12 = (bf16[64,192]{1,0:T(8,128)(2,1)S(1)}, bf16[64,192]{1,0:T(8,128)(2,1)S(1)}, u32[]{:S(2)}, u32[]{:S(2)}) collective-permute-start(bf16[64,192]{1,0:T(8,128)(2,1)S(1)} %get-tuple-element.40.q0), channel_id=1, source_target_pairs={{0,16},{8,24},{16,0},{24,8},{32,48},{40,56},{48,32},{56,40},{64,80... | collective-permute-start | bytes 73736 | tf_op jit(solution)/shard_map/ppermute | solution.py:424
  167.7 9.5 %copy-start.4 = (bf16[192,1536]{1,0:T(8,128)(2,1)S(1)}, bf16[192,1536]{1,0:T(8,128)(2,1)}, u32[]{:S(2)}) copy-start(bf16[192,1536]{1,0:T(8,128)(2,1)} %w.1) | copy-start | bytes 1769476
  169.2 5.0 %collective-permute-start.13 = (bf16[1,112,128]{2,1,0:T(8,128)(2,1)S(1)}, bf16[1,112,128]{2,1,0:T(8,128)(2,1)S(1)}, u32[]{:S(2)}, u32[]{:S(2)}) collective-permute-start(bf16[1,112,128]{2,1,0:T(8,128)(2,1)S(1)} %get-tuple-element.43), channel_id=1, source_target_pairs={{0,24},{8,0},{16,8},{24,16},{32,56},{40,32},{48,40},{56,48},{64,88... | collective-permute-start | bytes 86024 | tf_op jit(solution)/shard_map/ppermute | solution.py:424
  173.0 3.9 %collective-permute-start.14 = (bf16[1,112,128]{2,1,0:T(8,128)(2,1)S(1)}, bf16[1,112,128]{2,1,0:T(8,128)(2,1)S(1)}, u32[]{:S(2)}, u32[]{:S(2)}) collective-permute-start(bf16[1,112,128]{2,1,0:T(8,128)(2,1)S(1)} %get-tuple-element.42), channel_id=1, source_target_pairs={{0,8},{8,16},{16,24},{24,0},{32,40},{40,48},{48,56},{56,32},{64,72... | collective-permute-start | bytes 86024 | tf_op jit(solution)/shard_map/ppermute | solution.py:424
  173.0 4.2 %collective-permute-start.15 = (bf16[1,112,128]{2,1,0:T(8,128)(2,1)S(1)}, bf16[1,112,128]{2,1,0:T(8,128)(2,1)S(1)}, u32[]{:S(2)}, u32[]{:S(2)}) collective-permute-start(bf16[1,112,128]{2,1,0:T(8,128)(2,1)S(1)} %get-tuple-element.41), channel_id=1, source_target_pairs={{0,16},{8,24},{16,0},{24,8},{32,48},{40,56},{48,32},{56,40},{64,80... | collective-permute-start | bytes 86024 | tf_op jit(solution)/shard_map/ppermute | solution.py:424
